TPU v7x, 256 devices: a whole 4x4x8 slice. The times are simulated.
256 devices in a mesh: row: 16 (over z_hi, y), col: 16 (over x, z_lo, core).
Axes of the slice: x: 4, y: 4, z: 8 (z_hi: 4, z_lo: 2; z = z_hi * 2 + z_lo), core: 2. Of those that a mesh axis runs over, the one named last changes fastest.
Arguments:
- spectra: bfloat16 [8, 2, 512, 8192], P(None, None, 'col', 'row'), may hold values from -400 to 400, as said below
- channel_mask: int32 [8192], P('row'), may hold values 0 or 1
- pairing: int32 [16, 16], P('row'), may hold values from 0 to 15, each once within a row
Outputs:
- correlations: bfloat16 [256, 256, 8192], P('col', None, 'row')
Inputs may be any that keep to these rules, and one draw needn't show every extreme that they name: Each row of pairing names every block once. `spectra`: finite values of varying scale per segment, channel and frequency.
All inputs are finite; a program needn't handle non-finite values. No bound on the sum of `channel_mask` on one device may be relied on, other than what follows from the above.
Results may differ from a plain program's by a relative error of at most 0.0068.
Values may be sent and summed in bfloat16 or wider, within the bound.
No kernel may reach another device: no remote copies, remote signals or barrier semaphores. Data moves between devices by JAX's collectives and lax.ppermute only.
A program may use at most 128 MiB of HBM per device.

v0:
```python
import math

import jax
import jax.numpy as jnp
from jax import lax
from jax.sharding import PartitionSpec as P

BLOCK = 512
FREQ = 512
LAGS = 256
SOURCES = 16


def lag_kernel():
    lag_index = jnp.arange(LAGS, dtype=jnp.int32)
    freq_index = jnp.arange(FREQ, dtype=jnp.int32)
    phase_step = lag_index[:, None] * freq_index[None, :] % (2 * FREQ)
    angles = phase_step.astype(jnp.float32) * (math.pi / FREQ)
    weights = jnp.where(freq_index == 0, 0.5, 1.0).astype(jnp.float32) / math.sqrt(2.0 * FREQ)
    table = jnp.stack(
        [weights[None, :] * jnp.cos(angles), -weights[None, :] * jnp.sin(angles)], axis=1
    )
    return table.astype(jnp.bfloat16)


def cross_spectra(chosen, receiver):
    rotated = jnp.stack([-receiver[:, 1], receiver[:, 0]], axis=1)
    real_part = jnp.einsum("skfn,skfb->nfb", chosen, receiver, preferred_element_type=jnp.float32)
    imag_part = jnp.einsum("skfn,skfb->nfb", chosen, rotated, preferred_element_type=jnp.float32)
    return jnp.stack([real_part, imag_part], axis=1).astype(jnp.bfloat16)


def on_device(spectra, channel_mask, pairing):
    seg_count = spectra.shape[0]
    band_width = spectra.shape[2]
    blocks_all = lax.axis_size("row")
    group_size = blocks_all // lax.axis_size("col")
    masked = spectra.astype(jnp.float32) * channel_mask.astype(jnp.float32)[None, None, None, :]
    partial_energy = jnp.sum(masked * masked, axis=(1, 2))
    energy = lax.psum(partial_energy, "col") / FREQ
    whitened = (masked / jnp.sqrt(energy + 1e-06)[:, None, None, :]).astype(jnp.bfloat16)
    local_sources = whitened[..., :: BLOCK // SOURCES]
    gathered = lax.all_gather(local_sources, "row", axis=3, tiled=True)
    table = lag_kernel()
    order_row = pairing[0]
    chosen = jnp.take(
        gathered.reshape(seg_count, 2, band_width, blocks_all, SOURCES), order_row, axis=3
    )
    chosen = chosen.reshape(seg_count, 2, band_width, blocks_all * SOURCES)
    cross = cross_spectra(chosen, whitened).reshape(blocks_all, SOURCES, 2, band_width, BLOCK)
    lagged = jnp.einsum(
        "tkf,gvkfb->gvtb",
        table,
        lax.all_to_all(cross, "col", split_axis=0, concat_axis=3, tiled=True),
        preferred_element_type=jnp.float32,
    )
    lagged = lagged.astype(jnp.bfloat16)
    return lagged.reshape(group_size * SOURCES, LAGS, BLOCK)


def solution(mesh):
    in_specs = (P(None, None, "col", "row"), P("row"), P("row", None))
    out_specs = P("col", None, "row")
    return jax.shard_map(
        on_device, mesh=mesh, in_specs=in_specs, out_specs=out_specs, check_vma=False
    )
```

profile of v0, /device:TPU:17, one launch (start us, length us, event | category | flops | bytes accessed | tf_op | source)
XLA Modules:
  0.0 378.8 jit_solution(7282707620728337573)
XLA Ops:
  0.0 0.7 fusion.13
  0.7 0.7 compare_and_fusion
  1.3 0.7 convert_element_type.38
  2.0 1.3 multiply_reduce_fusion
  3.3 52.6 %psum.7 = f32[8,512]{1,0:T(8,128)S(1)} all-reduce(f32[8,512]{1,0:T(8,128)S(1)} %multiply_reduce_fusion), channel_id=1, replica_groups=mesh['row'=16,'col'=16] {'col'}, use_global_device_ids=true, to_apply=%region_1.0 | all-reduce | flops 4096 | bytes 32768 | tf_op jit(solution)/shard_map/psum | solution.py:40
  55.9 1.3 divide_convert_fusion
  57.3 3.5 slice.9
  61.0 41.2 %all_gather.3 = bf16[8,2,32,256]{2,0,1,3:T(8,128)(2,1)S(1)} all-gather(bf16[8,2,32,16]{2,0,1,3:T(8,128)(2,1)S(1)} %copy.17), channel_id=1, replica_groups=mesh['row'=16,'col'=16] {'row'}, dimensions={3}, use_global_device_ids=true | all-gather | bytes 278528 | tf_op jit(solution)/shard_map/all_gather | solution.py:43
  102.2 0.3 copy.18
  102.5 0.8 gather_fusion
  103.3 1.2 copy.19
  104.8 1.4 bitcast_select_fusion
  106.2 0.5 copy.20
  106.7 5.6 %bitcast_convert_fusion.1 = bf16[32,512,256]{1,2,0:T(8,128)(2,1)} fusion(bf16[8,2,32,512]{3,0,1,2:T(8,128)(2,1)S(1)} %divide_convert_fusion, bf16[8,2,32,256]{3,0,1,2:T(8,128)(2,1)S(1)} %copy.20), kind=kOutput, calls=%fused_computation.3 | convolution fusion | flops 138412032 | bytes 9175040 | tf_op jit(solution)/shard_map/skfn,skfb->nfb/dot_general | solution.py:28
  112.3 5.6 %bitcast_convert_fusion = bf16[32,512,256]{1,2,0:T(8,128)(2,1)} fusion(bf16[8,2,32,256]{3,0,1,2:T(8,128)(2,1)S(1)} %copy.20, bf16[8,1,32,512]{3,0,1,2:T(8,128)(2,1)S(1)} %get-tuple-element.6, bf16[8,1,32,512]{3,0,1,2:T(8,128)(2,1)S(1)} %get-tuple-element.5), kind=kOutput, calls=%fused_computation.2 | convolution fusion | flops 138674176 | bytes 9175040 | tf_op jit(solution)/shard_map/skfn,skfb->nfb/dot_general | solution.py:29
  117.8 12.3 %copy.23 = bf16[16,16,1,32,512]{4,3,2,1,0:T(8,128)(2,1)} copy(bf16[16,16,1,32,512]{4,1,0,3,2:T(8,128)(2,1)} %bitcast.46) | data formatting | bytes 16777216 | tf_op jit(solution)/shard_map/stack | solution.py:30
  130.2 12.5 %copy.22 = bf16[16,16,1,32,512]{4,3,2,1,0:T(8,128)(2,1)} copy(bf16[16,16,1,32,512]{4,1,0,3,2:T(8,128)(2,1)} %bitcast.45) | data formatting | bytes 16777216 | tf_op jit(solution)/shard_map/stack | solution.py:30
  142.6 13.8 %pad_maximum_fusion = bf16[16,16,2,32,512]{4,3,2,1,0:T(8,128)(2,1)} fusion(bf16[16,16,1,32,512]{4,3,2,1,0:T(8,128)(2,1)} %copy.23, bf16[16,16,1,32,512]{4,3,2,1,0:T(8,128)(2,1)} %copy.22), kind=kLoop, calls=%fused_computation.1 | loop fusion | flops 8388608 | bytes 33554432 | tf_op jit(solution)/shard_map/stack | solution.py:30
  156.4 16.6 %all-to-all-start = ((bf16[16,16,2,32,512]{4,3,2,1,0:T(8,128)(2,1)}), bf16[16,16,2,32,512]{4,3,2,1,0:T(8,128)(2,1)}, u32[]{:S(2)}, u32[]{:S(2)}) async-start(bf16[16,16,2,32,512]{4,3,2,1,0:T(8,128)(2,1)} %pad_maximum_fusion), calls=%async_computation | async-start | bytes 33554432 | tf_op jit(solution)/shard_map/all_to_all | solution.py:54
  173.0 2.2 multiply_convert_fusion
  175.3 182.3 %all-to-all-done = bf16[16,16,2,32,512]{4,3,2,1,0:T(8,128)(2,1)} async-done(((bf16[16,16,2,32,512]{4,3,2,1,0:T(8,128)(2,1)}), bf16[16,16,2,32,512]{4,3,2,1,0:T(8,128)(2,1)}, u32[]{:S(2)}, u32[]{:S(2)}) %all-to-all-start) | async-done | bytes 16777248 | tf_op jit(solution)/shard_map/all_to_all | solution.py:54
  357.6 8.4 %copy.24 = bf16[16,16,2,32,512]{4,3,0,2,1:T(8,128)(2,1)S(1)} copy(bf16[16,16,2,32,512]{4,3,2,1,0:T(8,128)(2,1)} %all-to-all-done) | data formatting | bytes 33554432 | tf_op jit(solution)/shard_map/all_to_all | solution.py:54
  366.0 6.4 %fusion = bf16[16,256,512]{1,2,0:T(8,128)(2,1)} fusion(bf16[16,2,512,512]{3,2,1,0:T(8,128)(2,1)S(1)} %bitcast.47, bf16[256,1,512]{2,0,1:T(8,128)(2,1)S(1)} %get-tuple-element.7, bf16[256,1,512]{2,0,1:T(8,128)(2,1)S(1)} %get-tuple-element.8), kind=kOutput, calls=%fused_computation.5 | convolution fusion | flops 4297326592 | bytes 21495808 | tf_op jit(solution)/shard_map/tkf,gvkfb->gvtb/dot_general | solution.py:51
  372.4 6.4 %copy.26 = bf16[16,256,512]{2,1,0:T(8,128)(2,1)} copy(bf16[16,256,512]{1,2,0:T(8,128)(2,1)} %fusion) | data formatting | bytes 8388608 | tf_op jit(solution)/shard_map/reshape | solution.py:58
  (8 shorter events, 0.4 us)
Async XLA Ops:
  156.4 201.2 %all-to-all-start = ((bf16[16,16,2,32,512]{4,3,2,1,0:T(8,128)(2,1)}), bf16[16,16,2,32,512]{4,3,2,1,0:T(8,128)(2,1)}, u32[]{:S(2)}, u32[]{:S(2)}) async-start(bf16[16,16,2,32,512]{4,3,2,1,0:T(8,128)(2,1)} %pad_maximum_fusion), calls=%async_computation | async-start | bytes 33554432 | tf_op jit(solution)/shard_map/all_to_all | solution.py:54
where the time goes:
time: 386 us; the launch traced here: 379 us
  waiting for transfers between devices  182 us (47%)
  blocking collectives  93.8 us (24%)
  local copies, waits for them, and re-layouts  46.2 us (12%)
  other arithmetic  22.2 us (6%)
  matrix products  17.5 us (5%)
  starting transfers between devices  16.6 us (4%)
    all_to_all x1, waiting for transfers between devices, on_device(): lax.all_to_all(cross, 'col', split_axis=0, concat_axis=3, tiled=True)  182 us
    psum x1, blocking collectives, on_device(): energy = lax.psum(partial_energy, 'col') / FREQ  52.6 us
    all_gather x1, blocking collectives, on_device(): gathered = lax.all_gather(local_sources, 'row', axis=3, tiled=True)  41.2 us
    another operation x2, local copies, waits for them, and re-layouts, cross_spectra(): return jnp.stack([real_part, imag_part], axis=1).astype(jnp.bfloat16)  24.8 us
    all_to_all x1, starting transfers between devices, on_device(): lax.all_to_all(cross, 'col', split_axis=0, concat_axis=3, tiled=True)  16.6 us
    another operation x1, other arithmetic, cross_spectra(): return jnp.stack([real_part, imag_part], axis=1).astype(jnp.bfloat16)  13.8 us
    all_to_all x1, local copies, waits for them, and re-layouts, on_device(): lax.all_to_all(cross, 'col', split_axis=0, concat_axis=3, tiled=True)  8.4 us
  transfers between devices with their start and end apart: 1, of which 1 were waited for; matrix products, arithmetic and copies ran while one was open for 1% of the time, Pallas kernels for 0%

commit v1 on v0

v1 whole, which is shorter than its diff:
```python
import math

import jax
import jax.numpy as jnp
import numpy as np
from jax import lax
from jax.experimental import pallas as pl
from jax.experimental.pallas import tpu as pltpu
from jax.sharding import PartitionSpec as P

BLOCK = 512
FREQ = 512
LAGS = 256
SEG = 8
SOURCES = 16
HALF = 16
STEP = BLOCK // SOURCES
GROUP = 2 * SEG * HALF
EPS = 1e-06
MIB = 1 << 20

BATCHES = (
    (
        ((0, 0, 0), (0, 0, 1)),
        ((1, 0, 0), (1, 0, 1)),
        ((3, 0, 0), (3, 0, 1)),
        ((0, 1, 0), (0, 1, 1)),
    ),
    (
        ((2, 0, 0), (1, 1, 1)),
        ((3, 1, 0), (2, 0, 1)),
        ((1, 1, 0), (3, 1, 1)),
    ),
    (
        ((2, 1, 0),),
        ((2, 1, 1),),
    ),
)


def ordered_groups(batch):
    return [(dx, dz, dc, half) for piece in batch for dc in (0, 1) for dx, dz, half in piece]


GROUPS = [group for batch in BATCHES for group in ordered_groups(batch)]


def dot(a, b, dims=((1,), (0,))):
    return lax.dot_general(a, b, (dims, ((), ())), preferred_element_type=jnp.float32)


def prepare_kernel(x_ref, mask_ref, out_ref):
    mask = mask_ref[...].astype(jnp.float32)
    row = lax.broadcasted_iota(jnp.int32, (SOURCES, BLOCK), 0)
    col = lax.broadcasted_iota(jnp.int32, (SOURCES, BLOCK), 1)
    pick = jnp.where(col == row * STEP, jnp.broadcast_to(mask, (SOURCES, BLOCK)), 0.0).astype(jnp.bfloat16)
    for half in range(2):
        part = x_ref[:, :, half * HALF : (half + 1) * HALF, :].reshape(GROUP, BLOCK)
        out_ref[0, :, half * GROUP : (half + 1) * GROUP] = dot(pick, part, ((1,), (1,))).astype(jnp.bfloat16)
    sums = []
    for seg in range(SEG):
        value = x_ref[seg].astype(jnp.float32).reshape(4 * HALF, BLOCK)
        sums.append(jnp.sum(value * value, axis=0, keepdims=True))
    energy = jnp.concatenate(sums, axis=0) * mask
    high = energy.astype(jnp.bfloat16).astype(jnp.float32)
    out_ref[1] = jnp.concatenate([high, energy - high], axis=0).astype(jnp.bfloat16)


def prepare(x, mask):
    return pl.pallas_call(
        prepare_kernel,
        out_shape=jax.ShapeDtypeStruct((2, SOURCES, BLOCK), jnp.bfloat16),
        compiler_params=pltpu.CompilerParams(vmem_limit_bytes=16 * MIB),
    )(x, mask)


def choose_kernel(index_ref, gathered_ref, out_ref):
    for slot in range(16):
        out_ref[slot] = gathered_ref[index_ref[slot]]


def choose(index, gathered):
    return pl.pallas_call(
        choose_kernel,
        out_shape=jax.ShapeDtypeStruct(gathered.shape, gathered.dtype),
        in_specs=[pl.BlockSpec(memory_space=pltpu.SMEM), pl.BlockSpec(memory_space=pltpu.VMEM)],
        compiler_params=pltpu.CompilerParams(vmem_limit_bytes=16 * MIB),
    )(index, gathered)


def scales_kernel(src_ref, energy_ref, mask_ref, scale_ref, white_ref):
    energy = jnp.zeros((SEG, BLOCK), jnp.float32)
    for n in range(16):
        both = energy_ref[n].astype(jnp.float32)
        energy = energy + (both[:SEG] + both[SEG:])
    mask = mask_ref[...].astype(jnp.float32)
    scale_ref[...] = mask * lax.rsqrt(energy / FREQ + EPS)

    power = jnp.zeros((SOURCES, 2 * GROUP), jnp.float32)
    for n in range(16):
        value = src_ref[n].astype(jnp.float32)
        power = power + value * value
    power = power[:, :GROUP] + power[:, GROUP:]
    row = lax.broadcasted_iota(jnp.int32, (GROUP, GROUP), 0)
    col = lax.broadcasted_iota(jnp.int32, (GROUP, GROUP), 1)
    same = jnp.where(row // (2 * HALF) == col // (2 * HALF), 1.0, 0.0)
    total = lax.dot_general(
        power, same, (((1,), (0,)), ((), ())), precision=lax.Precision.HIGHEST, preferred_element_type=jnp.float32
    )
    factor = lax.rsqrt(total / FREQ + EPS)
    turn = jnp.where(row == col + HALF, 1.0, 0.0) - jnp.where(row == col - HALF, 1.0, 0.0)
    first = (col // HALF) % 2 == 0
    turn = jnp.where(first, jnp.maximum(turn, 0.0), jnp.minimum(turn, 0.0)).astype(jnp.bfloat16)
    for g, (dx, dz, dc, half) in enumerate(GROUPS):
        n = (dc * 2 + dz) * 4 + dx
        value = src_ref[n, :, half * GROUP : (half + 1) * GROUP].astype(jnp.float32)
        real = (value * factor).astype(jnp.bfloat16)
        white_ref[g, :SOURCES] = real
        white_ref[g, SOURCES:] = dot(real, turn).astype(jnp.bfloat16)


def scales(src, energy, mask):
    return pl.pallas_call(
        scales_kernel,
        out_shape=(
            jax.ShapeDtypeStruct((SEG, BLOCK), jnp.float32),
            jax.ShapeDtypeStruct((len(GROUPS), 2 * SOURCES, GROUP), jnp.bfloat16),
        ),
        compiler_params=pltpu.CompilerParams(vmem_limit_bytes=16 * MIB),
    )(src, energy, mask)


def cross_kernel(count, first_group, halves, *refs):
    pieces, scale_ref, white_ref, out_ref, held = refs[:count], *refs[count:]
    for n, piece in enumerate(pieces):

        def whiten(seg, carry, n=n, piece=piece):
            factor = scale_ref[pl.ds(seg, 1), :].reshape(1, 1, BLOCK)
            value = (piece[seg].astype(jnp.float32) * factor).astype(jnp.bfloat16)
            for half in range(halves):
                part = value[:, half * HALF : (half + 1) * HALF, :].reshape(2 * HALF, BLOCK)
                held[n * halves + half, pl.ds(pl.multiple_of(seg * 2 * HALF, 2 * HALF), 2 * HALF), :] = part
            return carry

        lax.fori_loop(0, SEG, whiten, 0)

    lane = lax.broadcasted_iota(jnp.int32, (HALF, GROUP), 1)
    sub = lax.broadcasted_iota(jnp.int32, (HALF, GROUP), 0)
    diagonal = lane % HALF == sub

    def group(g, carry):
        white = white_ref[first_group + g].astype(jnp.float32)
        right = held[g]
        for quad in range(4):
            rows = []
            for v in range(quad * 4, quad * 4 + 4):
                for part in range(2):
                    one = white[part * SOURCES + v : part * SOURCES + v + 1, :]
                    rows.append(jnp.where(diagonal, jnp.broadcast_to(one, (HALF, GROUP)), 0.0))
            left = jnp.concatenate(rows, axis=0).astype(jnp.bfloat16)
            value = dot(left, right).astype(jnp.bfloat16).reshape(4, 2 * HALF, BLOCK)
            out_ref[quad * 4 : quad * 4 + 4, pl.ds(pl.multiple_of(g * 2 * HALF, 2 * HALF), 2 * HALF), :] = value
        return carry

    lax.fori_loop(0, count * halves, group, 0)


def cross(pieces, scale, white, first_group):
    halves = pieces[0].shape[2] // HALF
    groups = len(pieces) * halves

    def kernel(*refs):
        cross_kernel(len(pieces), first_group, halves, *refs)

    return pl.pallas_call(
        kernel,
        out_shape=jax.ShapeDtypeStruct((SOURCES, groups * 2 * HALF, BLOCK), jnp.bfloat16),
        scratch_shapes=[pltpu.VMEM((groups, GROUP, BLOCK), jnp.bfloat16)],
        compiler_params=pltpu.CompilerParams(vmem_limit_bytes=40 * MIB),
        cost_estimate=pl.CostEstimate(
            flops=groups * 2 * 512 * 256 * 512, bytes_accessed=groups * 512 * 1024, transcendentals=0
        ),
    )(*pieces, scale, white)


def lag_kernel(table_ref, *refs):
    *cross_refs, out_ref = refs
    total, start = None, 0
    for ref in cross_refs:
        rows = ref.shape[1]
        term = dot(table_ref[:, start : start + rows], ref[0])
        total = term if total is None else total + term
        start += rows
    out_ref[0] = total.astype(jnp.bfloat16)


def lag(table, parts):
    return pl.pallas_call(
        lag_kernel,
        grid=(SOURCES,),
        out_shape=jax.ShapeDtypeStruct((SOURCES, LAGS, BLOCK), jnp.bfloat16),
        in_specs=[pl.BlockSpec((LAGS, 2 * FREQ), lambda v: (0, 0))]
        + [pl.BlockSpec((1, part.shape[1], BLOCK), lambda v: (v, 0, 0)) for part in parts],
        out_specs=pl.BlockSpec((1, LAGS, BLOCK), lambda v: (v, 0, 0)),
        compiler_params=pltpu.CompilerParams(vmem_limit_bytes=32 * MIB),
    )(table, *parts)


def lag_table(ix, iz, ic):
    dx, dz, dc, half = (np.array([g[i] for g in GROUPS], np.int32) for i in range(4))
    spread = lambda a: np.repeat(a, 2 * HALF)
    part = np.tile(np.repeat(np.arange(2, dtype=np.int32), HALF), len(GROUPS))
    inner = np.tile(np.arange(HALF, dtype=np.int32), 2 * len(GROUPS)) + HALF * spread(half)
    place = ((ix + 4 - spread(dx)) % 4) * 4 + (iz ^ spread(dz)) * 2 + (ic ^ spread(dc))
    freq = (place * 2 * HALF + inner)[None, :]
    time = lax.broadcasted_iota(jnp.int32, (LAGS, 2 * FREQ), 0)
    phase = (time * freq + part[None, :] * (FREQ // 2)) % (2 * FREQ)
    weight = jnp.where(freq == 0, 0.5, 1.0).astype(jnp.float32) / math.sqrt(2.0 * FREQ)
    return (weight * jnp.cos(phase.astype(jnp.float32) * (math.pi / FREQ))).astype(jnp.bfloat16)


def send(value, axis, where):
    return lax.ppermute(value, axis, [(n, where(n)) for n in range(16)])


def on_slow(n, d):
    return (n // 4 + d) % 4 * 4 + n % 4


def on_fast(n, d):
    return n // 4 * 4 + (n % 4 + d) % 4


def on_device(x, mask, pairing):
    row, col = lax.axis_index("row"), lax.axis_index("col")
    iz_hi, iy = row // 4, row % 4
    ix, iz, ic = col // 4, col // 2 % 2, col % 2
    up = lambda v: send(v, "col", lambda n: on_slow(n, 1))
    down = lambda v: send(v, "col", lambda n: on_slow(n, -1))
    across = lambda v: send(v, "col", lambda n: n ^ 2)
    sibling = lambda v: send(v, "col", lambda n: n ^ 1)
    low = lambda v: v[:, :, :HALF]
    high = lambda v: v[:, :, HALF:]
    join = lambda a, b: jnp.concatenate([a, b], axis=2)

    a1, b1, c1 = up(x), down(x), across(x)
    a2 = up(join(low(a1), high(c1)))
    b2 = down(join(low(c1), high(b1)))
    c2 = across(join(low(a1), high(b1)))
    a3 = up(high(a2))
    b3 = down(low(b2))

    mask_row = mask.reshape(1, BLOCK)
    prepared = prepare(x, mask_row)
    own, partial = prepared[:1], prepared[1:]
    by_y = jnp.concatenate([own] + [send(own, "row", lambda n, d=d: on_fast(n, d)) for d in (1, 2, 3)])
    by_row = jnp.concatenate([by_y] + [send(by_y, "row", lambda n, d=d: on_slow(n, d)) for d in (1, 2, 3)])
    slot = np.arange(16, dtype=np.int32)
    target = (ix + slot // 4) % 4 * 4 + (iz ^ (slot // 2 % 2)) * 2 + (ic ^ (slot % 2))
    block = pairing[0][target]
    index = (iz_hi + 4 - block // 4) % 4 * 4 + (iy + 4 - block % 4) % 4
    chosen = choose(index, by_row).reshape(4, 2, 2, SOURCES, BLOCK)

    def flat(parts):
        return jnp.concatenate([part.reshape(-1, SOURCES, BLOCK) for part in parts])

    got = [flat([chosen[0], partial])]
    got += [send(flat([chosen[d], partial]), "col", lambda n, d=d: on_slow(n, d)) for d in (1, 2, 3)]
    got = jnp.stack(got)
    src, energy = got[:, :4].reshape(4, 2, 2, SOURCES, BLOCK), got[:, 4]
    other = across(flat([src[:, 1], energy]))
    src = jnp.stack([src[:, 0], other[:8].reshape(4, 2, SOURCES, BLOCK)])
    energy = jnp.stack([energy, other[8:]])
    other = sibling(flat([src[:, :, 1], energy]))
    src = flat([src[:, :, 0], other[:8]])
    energy = flat([energy, other[8:]])
    scale, white = scales(src, energy, mask_row)

    table = lag_table(ix, iz, ic)
    parts, first = [], 0
    for batch, pieces in zip(BATCHES, ((x, a1, b1, c1), (a2, b2, c2), (b3, a3)), strict=True):
        both = [piece for mine in pieces for piece in (mine, sibling(mine))]
        parts.append(cross(both, scale, white, first))
        first += len(ordered_groups(batch))
    return lag(table, parts)


def solution(mesh):
    in_specs = (P(None, None, "col", "row"), P("row"), P("row", None))
    out_specs = P("col", None, "row")
    return jax.shard_map(on_device, mesh=mesh, in_specs=in_specs, out_specs=out_specs, check_vma=False)
```

time: 386 us -> 103 us (0.27)
  the two profiles are of different devices: /device:TPU:17 before, /device:TPU:1 now
where the time goes in v1:
time: 103 us; the launch traced here: 102 us
  starting transfers between devices  53.3 us (52%)
  Pallas kernels  24.3 us (24%)
  waiting for transfers between devices  11.1 us (11%)
  local copies, waits for them, and re-layouts  8.13 us (8%)
  other arithmetic  5.19 us (5%)
    ppermute x28, starting transfers between devices, send(): return lax.ppermute(value, axis, [(n, where(n)) for n in range(16)])  53.3 us
    pallas_call x3, Pallas kernels, cross(): pl.pallas_call(kernel, out_shape=jax.ShapeDtypeStruct((SOURCES, groups *...  12.1 us
    ppermute x28, waiting for transfers between devices, send(): return lax.ppermute(value, axis, [(n, where(n)) for n in range(16)])  11.1 us
    pallas_call x1, Pallas kernels, lag(): pl.pallas_call(lag_kernel, grid=(SOURCES,), out_shape=jax.ShapeDtypeStruc...  10.2 us
    unnamed x30, local copies, waits for them, and re-layouts  7.26 us
    convert_element_type x1, other arithmetic, lag_table(): (weight * jnp.cos(phase.astype(jnp.float32) * (math.pi / FREQ))).astype(j...  4.01 us
  transfers between devices with their start and end apart: 28, of which 8 were waited for; matrix products, arithmetic and copies ran while one was open for 6% of the time, Pallas kernels for 11%

profile of v1, /device:TPU:1, one launch (start us, length us, event | category | flops | bytes accessed | tf_op | source)
XLA Modules:
  0.0 102.4 jit_solution(2565399929073884047)
XLA Ops:
  2.0 2.1 %collective-permute-start.7 = (bf16[1,16,512]{2,1,0:T(8,128)(2,1)S(1)}, bf16[1,16,512]{2,1,0:T(8,128)(2,1)S(1)}, u32[]{:S(2)}, u32[]{:S(2)}) collective-permute-start(bf16[1,16,512]{2,1,0:T(8,128)(2,1)S(1)} %get-tuple-element.26), channel_id=1, source_target_pairs={{0,16},{16,32},{32,48},{48,0},{64,80},{80,96},{96,112},{112,64},{1... | collective-permute-start | bytes 49160 | tf_op jit(solution)/shard_map/ppermute | solution.py:223
  4.2 2.6 %collective-permute-start.8 = (bf16[1,16,512]{2,1,0:T(8,128)(2,1)S(1)}, bf16[1,16,512]{2,1,0:T(8,128)(2,1)S(1)}, u32[]{:S(2)}, u32[]{:S(2)}) collective-permute-start(bf16[1,16,512]{2,1,0:T(8,128)(2,1)S(1)} %get-tuple-element.26), channel_id=1, source_target_pairs={{0,32},{16,48},{32,0},{48,16},{64,96},{80,112},{96,64},{112,80},{1... | collective-permute-start | bytes 49160 | tf_op jit(solution)/shard_map/ppermute | solution.py:223
  9.7 3.1 %collective-permute-start.10 = (bf16[4,16,512]{2,1,0:T(8,128)(2,1)S(1)}, bf16[4,16,512]{2,1,0:T(8,128)(2,1)S(1)}, u32[]{:S(2)}, u32[]{:S(2)}) collective-permute-start(bf16[4,16,512]{2,1,0:T(8,128)(2,1)S(1)} %pad_maximum_fusion.15), channel_id=1, source_target_pairs={{0,64},{16,80},{32,96},{48,112},{64,128},{80,144},{96,160},{112,17... | collective-permute-start | bytes 196616 | tf_op jit(solution)/shard_map/ppermute | solution.py:223
  12.7 5.1 %collective-permute-start.11 = (bf16[4,16,512]{2,1,0:T(8,128)(2,1)S(1)}, bf16[4,16,512]{2,1,0:T(8,128)(2,1)S(1)}, u32[]{:S(2)}, u32[]{:S(2)}) collective-permute-start(bf16[4,16,512]{2,1,0:T(8,128)(2,1)S(1)} %pad_maximum_fusion.15), channel_id=1, source_target_pairs={{0,128},{16,144},{32,160},{48,176},{64,192},{80,208},{96,224},{112... | collective-permute-start | bytes 196616 | tf_op jit(solution)/shard_map/ppermute | solution.py:223
  17.9 2.4 %collective-permute-start.12 = (bf16[4,16,512]{2,1,0:T(8,128)(2,1)S(1)}, bf16[4,16,512]{2,1,0:T(8,128)(2,1)S(1)}, u32[]{:S(2)}, u32[]{:S(2)}) collective-permute-start(bf16[4,16,512]{2,1,0:T(8,128)(2,1)S(1)} %pad_maximum_fusion.15), channel_id=1, source_target_pairs={{0,192},{16,208},{32,224},{48,240},{64,0},{80,16},{96,32},{112,48}... | collective-permute-start | bytes 196616 | tf_op jit(solution)/shard_map/ppermute | solution.py:223
  20.5 2.3 %collective-permute-done.12 = bf16[4,16,512]{2,1,0:T(8,128)(2,1)S(1)} collective-permute-done((bf16[4,16,512]{2,1,0:T(8,128)(2,1)S(1)}, bf16[4,16,512]{2,1,0:T(8,128)(2,1)S(1)}, u32[]{:S(2)}, u32[]{:S(2)}) %collective-permute-start.12) | collective-permute-done | bytes 65568 | tf_op jit(solution)/shard_map/ppermute | solution.py:223
  23.5 1.3 %collective-permute-start.13 = (bf16[5,16,512]{2,1,0:T(8,128)(2,1)S(1)}, bf16[5,16,512]{2,1,0:T(8,128)(2,1)S(1)}, u32[]{:S(2)}, u32[]{:S(2)}) collective-permute-start(bf16[5,16,512]{2,1,0:T(8,128)(2,1)S(1)} %get-tuple-element.30), channel_id=1, source_target_pairs={{0,4},{1,5},{2,6},{3,7},{4,8},{5,9},{6,10},{7,11},{8,12},{9,13},{1... | collective-permute-start | bytes 245768 | tf_op jit(solution)/shard_map/ppermute | solution.py:223
  24.8 2.5 %collective-permute-start.14 = (bf16[5,16,512]{2,1,0:T(8,128)(2,1)S(1)}, bf16[5,16,512]{2,1,0:T(8,128)(2,1)S(1)}, u32[]{:S(2)}, u32[]{:S(2)}) collective-permute-start(bf16[5,16,512]{2,1,0:T(8,128)(2,1)S(1)} %get-tuple-element.31), channel_id=1, source_target_pairs={{0,8},{1,9},{2,10},{3,11},{4,12},{5,13},{6,14},{7,15},{8,0},{9,1},... | collective-permute-start | bytes 245768 | tf_op jit(solution)/shard_map/ppermute | solution.py:223
  29.6 2.4 %collective-permute-start.3 = (bf16[8,2,32,512]{3,2,1,0:T(8,128)(2,1)}, bf16[8,2,32,512]{3,2,1,0:T(8,128)(2,1)S(1)}, u32[]{:S(2)}, u32[]{:S(2)}) collective-permute-start(bf16[8,2,32,512]{3,2,1,0:T(8,128)(2,1)} %refs_0_.1), channel_id=1, source_target_pairs={{0,12},{1,13},{2,14},{3,15},{4,0},{5,1},{6,2},{7,3},{8,4},{9,5},{1... | collective-permute-start | bytes 1572872 | tf_op jit(solution)/shard_map/ppermute | solution.py:223
  32.0 5.5 %collective-permute-start = (bf16[8,2,32,512]{3,2,1,0:T(8,128)(2,1)}, bf16[8,2,32,512]{3,2,1,0:T(8,128)(2,1)S(1)}, u32[]{:S(2)}, u32[]{:S(2)}) collective-permute-start(bf16[8,2,32,512]{3,2,1,0:T(8,128)(2,1)} %refs_0_.1), channel_id=1, source_target_pairs={{0,1},{1,0},{2,3},{3,2},{4,5},{5,4},{6,7},{7,6},{8,9},{9,8},{10,11... | collective-permute-start | bytes 1572872 | tf_op jit(solution)/shard_map/ppermute | solution.py:223
  38.5 2.4 %collective-permute-done.1.refs_2_ = bf16[8,2,32,512]{3,2,1,0:T(8,128)(2,1)S(1)} collective-permute-done((bf16[8,2,32,512]{3,2,1,0:T(8,128)(2,1)}, bf16[8,2,32,512]{3,2,1,0:T(8,128)(2,1)S(1)}, u32[]{:S(2)}, u32[]{:S(2)}) %collective-permute-start.1) | collective-permute-done | bytes 524320 | tf_op jit(solution)/shard_map/ppermute | solution.py:223
  41.7 2.7 %collective-permute-start.20 = (bf16[8,2,32,512]{3,2,1,0:T(8,128)(2,1)S(1)}, bf16[8,2,32,512]{3,2,1,0:T(8,128)(2,1)S(1)}, u32[]{:S(2)}, u32[]{:S(2)}) collective-permute-start(bf16[8,2,32,512]{3,2,1,0:T(8,128)(2,1)S(1)} %get-tuple-element.14), channel_id=1, source_target_pairs={{0,12},{1,13},{2,14},{3,15},{4,0},{5,1},{6,2},{7,3},{8,4},{9,5},{1... | collective-permute-start | bytes 1572872 | tf_op jit(solution)/shard_map/ppermute | solution.py:223
  45.8 5.3 %collective-permute-start.2 = (bf16[8,2,32,512]{3,2,1,0:T(8,128)(2,1)S(1)}, bf16[8,2,32,512]{3,2,1,0:T(8,128)(2,1)S(1)}, u32[]{:S(2)}, u32[]{:S(2)}) collective-permute-start(bf16[8,2,32,512]{3,2,1,0:T(8,128)(2,1)S(1)} %collective-permute-done.1.refs_2_), channel_id=1, source_target_pairs={{0,1},{1,0},{2,3},{3,2},{4,5},{5,4},{6,7},{7,6},{8,9},{9,8},{10,11... | collective-permute-start | bytes 1572872 | tf_op jit(solution)/shard_map/ppermute | solution.py:223
  51.9 5.3 %collective-permute-start.6 = (bf16[8,2,32,512]{3,2,1,0:T(8,128)(2,1)S(1)}, bf16[8,2,32,512]{3,2,1,0:T(8,128)(2,1)S(1)}, u32[]{:S(2)}, u32[]{:S(2)}) collective-permute-start(bf16[8,2,32,512]{3,2,1,0:T(8,128)(2,1)S(1)} %collective-permute-done.5.refs_6_), channel_id=1, source_target_pairs={{0,1},{1,0},{2,3},{3,2},{4,5},{5,4},{6,7},{7,6},{8,9},{9,8},{10,11... | collective-permute-start | bytes 1572872 | tf_op jit(solution)/shard_map/ppermute | solution.py:223
  57.2 3.0 %collective-permute-start.17 = (bf16[16,16,512]{2,1,0:T(8,128)(2,1)S(1)}, bf16[16,16,512]{2,1,0:T(8,128)(2,1)S(1)}, u32[]{:S(2)}, u32[]{:S(2)}) collective-permute-start(bf16[16,16,512]{2,1,0:T(8,128)(2,1)S(1)} %pad_maximum_fusion.4), channel_id=1, source_target_pairs={{0,1},{1,0},{2,3},{3,2},{4,5},{5,4},{6,7},{7,6},{8,9},{9,8},{10,11... | collective-permute-start | bytes 786440 | tf_op jit(solution)/shard_map/ppermute | solution.py:223
  60.2 4.0 %fusion.5.table_ref = bf16[256,1024]{1,0:T(8,128)(2,1)S(1)} fusion(s32[1024]{0:T(1024)S(1)} %copy-done.7, s32[1024]{0:T(1024)S(1)} %get-tuple-element.10, f32[1024]{0:T(1024)S(1)} %get-tuple-element.9), kind=kLoop, calls=%fused_computation.9 | loop fusion | flops 4456448 | bytes 536576 | tf_op jit(solution)/shard_map/convert_element_type | solution.py:219
  68.2 4.1 %collective-permute-done.24.refs_0_ = bf16[8,2,16,512]{3,2,1,0:T(8,128)(2,1)S(1)} collective-permute-done((bf16[8,2,16,512]{3,2,1,0:T(8,128)(2,1)S(1)}, bf16[8,2,16,512]{3,2,1,0:T(8,128)(2,1)S(1)}, u32[]{:S(2)}, u32[]{:S(2)}) %collective-permute-start.24) | collective-permute-done | bytes 262176 | tf_op jit(solution)/shard_map/ppermute | solution.py:223
  73.1 1.4 %collective-permute-start.27 = (bf16[8,2,16,512]{3,2,1,0:T(8,128)(2,1)S(1)}, bf16[8,2,16,512]{3,2,1,0:T(8,128)(2,1)S(1)}, u32[]{:S(2)}, u32[]{:S(2)}) collective-permute-start(bf16[8,2,16,512]{3,2,1,0:T(8,128)(2,1)S(1)} %collective-permute-done.26.refs_2_), channel_id=1, source_target_pairs={{0,1},{1,0},{2,3},{3,2},{4,5},{5,4},{6,7},{7,6},{8,9},{9,8},{10,11... | collective-permute-start | bytes 786440 | tf_op jit(solution)/shard_map/ppermute | solution.py:223
  74.6 6.0 %shard_map.112.refs_0_ = bf16[16,512,512]{2,1,0:T(8,128)(2,1)S(1)} custom-call(bf16[8,2,32,512]{3,2,1,0:T(8,128)(2,1)S(1)} %copy-done.4, bf16[8,2,32,512]{3,2,1,0:T(8,128)(2,1)S(1)} %collective-permute-done.refs_1_, bf16[8,2,32,512]{3,2,1,0:T(8,128)(2,1)S(1)} %collective-permute-done.1.refs_2_, bf16[8,2,32,512]{3,2,1,0:T(8,128)(2,1)S(1)} %collective-permute-done.2.refs_3_, ...), custom_call_target="tpu_custom_call" | custom-call | flops 2147483648 | bytes 8388608 | tf_op jit(solution)/shard_map/pallas_call | solution.py:175
  80.6 4.6 %shard_map.113.refs_1_ = bf16[16,384,512]{2,1,0:T(8,128)(2,1)S(1)} custom-call(bf16[8,2,32,512]{3,2,1,0:T(8,128)(2,1)S(1)} %collective-permute-done.18.refs_0_, bf16[8,2,32,512]{3,2,1,0:T(8,128)(2,1)S(1)} %collective-permute-done.19.refs_1_, bf16[8,2,32,512]{3,2,1,0:T(8,128)(2,1)S(1)} %collective-permute-done.20.refs_2_, ...), custom_call_target="tpu_custom_call" | custom-call | flops 1610612736 | bytes 6291456 | tf_op jit(solution)/shard_map/pallas_call | solution.py:175
  85.2 2.7 %copy-done.1 = bf16[16,384,512]{2,1,0:T(8,128)(2,1)} copy-done((bf16[16,384,512]{2,1,0:T(8,128)(2,1)}, bf16[16,384,512]{2,1,0:T(8,128)(2,1)S(1)}, u32[]{:S(2)}) %copy-start.1) | copy-done | bytes 6291480
  87.9 1.6 %shard_map.114.refs_2_ = bf16[16,128,512]{2,1,0:T(8,128)(2,1)S(1)} custom-call(bf16[8,2,16,512]{3,2,1,0:T(8,128)(2,1)S(1)} %collective-permute-done.24.refs_0_, bf16[8,2,16,512]{3,2,1,0:T(8,128)(2,1)S(1)} %collective-permute-done.25.refs_1_, bf16[8,2,16,512]{3,2,1,0:T(8,128)(2,1)S(1)} %collective-permute-done.26.refs_2_, ...), custom_call_target="tpu_custom_call" | custom-call | flops 536870912 | bytes 2097152 | tf_op jit(solution)/shard_map/pallas_call | solution.py:175
  89.5 2.8 %copy-done.2 = bf16[16,384,512]{2,1,0:T(8,128)(2,1)S(1)} copy-done((bf16[16,384,512]{2,1,0:T(8,128)(2,1)S(1)}, bf16[16,384,512]{2,1,0:T(8,128)(2,1)}, u32[]{:S(2)}) %copy-start.2) | copy-done | bytes 6291480
  92.2 10.2 %shard_map.115 = bf16[16,256,512]{2,1,0:T(8,128)(2,1)} custom-call(bf16[256,1024]{1,0:T(8,128)(2,1)S(1)} %fusion.5.table_ref, bf16[16,512,512]{2,1,0:T(8,128)(2,1)S(1)} %shard_map.112.refs_0_, bf16[16,384,512]{2,1,0:T(8,128)(2,1)S(1)} %copy-done.2, bf16[16,128,512]{2,1,0:T(8,128)(2,1)S(1)} %shard_map.114.refs_2_), custom_call_target="tpu_custom_call" | custom-call | tf_op jit(solution)/shard_map/pallas_call | solution.py:198
  (98 shorter events, 16.6 us)
Async XLA Ops:
  2.0 7.3 %collective-permute-start.7 = (bf16[1,16,512]{2,1,0:T(8,128)(2,1)S(1)}, bf16[1,16,512]{2,1,0:T(8,128)(2,1)S(1)}, u32[]{:S(2)}, u32[]{:S(2)}) collective-permute-start(bf16[1,16,512]{2,1,0:T(8,128)(2,1)S(1)} %get-tuple-element.26), channel_id=1, source_target_pairs={{0,16},{16,32},{32,48},{48,0},{64,80},{80,96},{96,112},{112,64},{1... | collective-permute-start | bytes 49160 | tf_op jit(solution)/shard_map/ppermute | solution.py:223
  9.7 10.6 %collective-permute-start.10 = (bf16[4,16,512]{2,1,0:T(8,128)(2,1)S(1)}, bf16[4,16,512]{2,1,0:T(8,128)(2,1)S(1)}, u32[]{:S(2)}, u32[]{:S(2)}) collective-permute-start(bf16[4,16,512]{2,1,0:T(8,128)(2,1)S(1)} %pad_maximum_fusion.15), channel_id=1, source_target_pairs={{0,64},{16,80},{32,96},{48,112},{64,128},{80,144},{96,160},{112,17... | collective-permute-start | bytes 196616 | tf_op jit(solution)/shard_map/ppermute | solution.py:223
  12.7 7.8 %collective-permute-start.11 = (bf16[4,16,512]{2,1,0:T(8,128)(2,1)S(1)}, bf16[4,16,512]{2,1,0:T(8,128)(2,1)S(1)}, u32[]{:S(2)}, u32[]{:S(2)}) collective-permute-start(bf16[4,16,512]{2,1,0:T(8,128)(2,1)S(1)} %pad_maximum_fusion.15), channel_id=1, source_target_pairs={{0,128},{16,144},{32,160},{48,176},{64,192},{80,208},{96,224},{112... | collective-permute-start | bytes 196616 | tf_op jit(solution)/shard_map/ppermute | solution.py:223
  24.8 7.2 %collective-permute-start.14 = (bf16[5,16,512]{2,1,0:T(8,128)(2,1)S(1)}, bf16[5,16,512]{2,1,0:T(8,128)(2,1)S(1)}, u32[]{:S(2)}, u32[]{:S(2)}) collective-permute-start(bf16[5,16,512]{2,1,0:T(8,128)(2,1)S(1)} %get-tuple-element.31), channel_id=1, source_target_pairs={{0,8},{1,9},{2,10},{3,11},{4,12},{5,13},{6,14},{7,15},{8,0},{9,1},... | collective-permute-start | bytes 245768 | tf_op jit(solution)/shard_map/ppermute | solution.py:223
  27.2 10.3 %collective-permute-start.15 = (bf16[5,16,512]{2,1,0:T(8,128)(2,1)S(1)}, bf16[5,16,512]{2,1,0:T(8,128)(2,1)S(1)}, u32[]{:S(2)}, u32[]{:S(2)}) collective-permute-start(bf16[5,16,512]{2,1,0:T(8,128)(2,1)S(1)} %get-tuple-element.32), channel_id=1, source_target_pairs={{0,12},{1,13},{2,14},{3,15},{4,0},{5,1},{6,2},{7,3},{8,4},{9,5},{1... | collective-permute-start | bytes 245768 | tf_op jit(solution)/shard_map/ppermute | solution.py:223
  28.4 10.1 %collective-permute-start.5 = (bf16[8,2,32,512]{3,2,1,0:T(8,128)(2,1)}, bf16[8,2,32,512]{3,2,1,0:T(8,128)(2,1)S(1)}, u32[]{:S(2)}, u32[]{:S(2)}) collective-permute-start(bf16[8,2,32,512]{3,2,1,0:T(8,128)(2,1)} %refs_0_.1), channel_id=1, source_target_pairs={{0,2},{1,3},{2,0},{3,1},{4,6},{5,7},{6,4},{7,5},{8,10},{9,11},{10,... | collective-permute-start | bytes 1572872 | tf_op jit(solution)/shard_map/ppermute | solution.py:223
  29.3 11.6 %collective-permute-start.1 = (bf16[8,2,32,512]{3,2,1,0:T(8,128)(2,1)}, bf16[8,2,32,512]{3,2,1,0:T(8,128)(2,1)S(1)}, u32[]{:S(2)}, u32[]{:S(2)}) collective-permute-start(bf16[8,2,32,512]{3,2,1,0:T(8,128)(2,1)} %refs_0_.1), channel_id=1, source_target_pairs={{0,4},{1,5},{2,6},{3,7},{4,8},{5,9},{6,10},{7,11},{8,12},{9,13},{1... | collective-permute-start | bytes 1572872 | tf_op jit(solution)/shard_map/ppermute | solution.py:223
  29.6 11.9 %collective-permute-start.3 = (bf16[8,2,32,512]{3,2,1,0:T(8,128)(2,1)}, bf16[8,2,32,512]{3,2,1,0:T(8,128)(2,1)S(1)}, u32[]{:S(2)}, u32[]{:S(2)}) collective-permute-start(bf16[8,2,32,512]{3,2,1,0:T(8,128)(2,1)} %refs_0_.1), channel_id=1, source_target_pairs={{0,12},{1,13},{2,14},{3,15},{4,0},{5,1},{6,2},{7,3},{8,4},{9,5},{1... | collective-permute-start | bytes 1572872 | tf_op jit(solution)/shard_map/ppermute | solution.py:223
  32.0 19.1 %collective-permute-start = (bf16[8,2,32,512]{3,2,1,0:T(8,128)(2,1)}, bf16[8,2,32,512]{3,2,1,0:T(8,128)(2,1)S(1)}, u32[]{:S(2)}, u32[]{:S(2)}) collective-permute-start(bf16[8,2,32,512]{3,2,1,0:T(8,128)(2,1)} %refs_0_.1), channel_id=1, source_target_pairs={{0,1},{1,0},{2,3},{3,2},{4,5},{5,4},{6,7},{7,6},{8,9},{9,8},{10,11... | collective-permute-start | bytes 1572872 | tf_op jit(solution)/shard_map/ppermute | solution.py:223
  37.7 7.1 %collective-permute-start.16 = (bf16[12,16,512]{2,1,0:T(8,128)(2,1)S(1)}, bf16[12,16,512]{2,1,0:T(8,128)(2,1)S(1)}, u32[]{:S(2)}, u32[]{:S(2)}) collective-permute-start(bf16[12,16,512]{2,1,0:T(8,128)(2,1)S(1)} %pad_maximum_fusion.7), channel_id=1, source_target_pairs={{0,2},{1,3},{2,0},{3,1},{4,6},{5,7},{6,4},{7,5},{8,10},{9,11},{10,... | collective-permute-start | bytes 589832 | tf_op jit(solution)/shard_map/ppermute | solution.py:223
  41.7 10.2 %collective-permute-start.20 = (bf16[8,2,32,512]{3,2,1,0:T(8,128)(2,1)S(1)}, bf16[8,2,32,512]{3,2,1,0:T(8,128)(2,1)S(1)}, u32[]{:S(2)}, u32[]{:S(2)}) collective-permute-start(bf16[8,2,32,512]{3,2,1,0:T(8,128)(2,1)S(1)} %get-tuple-element.14), channel_id=1, source_target_pairs={{0,12},{1,13},{2,14},{3,15},{4,0},{5,1},{6,2},{7,3},{8,4},{9,5},{1... | collective-permute-start | bytes 1572872 | tf_op jit(solution)/shard_map/ppermute | solution.py:223
  44.4 12.7 %collective-permute-start.18 = (bf16[8,2,32,512]{3,2,1,0:T(8,128)(2,1)S(1)}, bf16[8,2,32,512]{3,2,1,0:T(8,128)(2,1)S(1)}, u32[]{:S(2)}, u32[]{:S(2)}) collective-permute-start(bf16[8,2,32,512]{3,2,1,0:T(8,128)(2,1)S(1)} %get-tuple-element.15), channel_id=1, source_target_pairs={{0,4},{1,5},{2,6},{3,7},{4,8},{5,9},{6,10},{7,11},{8,12},{9,13},{1... | collective-permute-start | bytes 1572872 | tf_op jit(solution)/shard_map/ppermute | solution.py:223
  44.8 19.8 %collective-permute-start.22 = (bf16[8,2,32,512]{3,2,1,0:T(8,128)(2,1)S(1)}, bf16[8,2,32,512]{3,2,1,0:T(8,128)(2,1)S(1)}, u32[]{:S(2)}, u32[]{:S(2)}) collective-permute-start(bf16[8,2,32,512]{3,2,1,0:T(8,128)(2,1)S(1)} %get-tuple-element.13), channel_id=1, source_target_pairs={{0,2},{1,3},{2,0},{3,1},{4,6},{5,7},{6,4},{7,5},{8,10},{9,11},{10,... | collective-permute-start | bytes 1572872 | tf_op jit(solution)/shard_map/ppermute | solution.py:223
  45.8 20.1 %collective-permute-start.2 = (bf16[8,2,32,512]{3,2,1,0:T(8,128)(2,1)S(1)}, bf16[8,2,32,512]{3,2,1,0:T(8,128)(2,1)S(1)}, u32[]{:S(2)}, u32[]{:S(2)}) collective-permute-start(bf16[8,2,32,512]{3,2,1,0:T(8,128)(2,1)S(1)} %collective-permute-done.1.refs_2_), channel_id=1, source_target_pairs={{0,1},{1,0},{2,3},{3,2},{4,5},{5,4},{6,7},{7,6},{8,9},{9,8},{10,11... | collective-permute-start | bytes 1572872 | tf_op jit(solution)/shard_map/ppermute | solution.py:223
  51.1 15.4 %collective-permute-start.4 = (bf16[8,2,32,512]{3,2,1,0:T(8,128)(2,1)S(1)}, bf16[8,2,32,512]{3,2,1,0:T(8,128)(2,1)S(1)}, u32[]{:S(2)}, u32[]{:S(2)}) collective-permute-start(bf16[8,2,32,512]{3,2,1,0:T(8,128)(2,1)S(1)} %collective-permute-done.3.refs_4_), channel_id=1, source_target_pairs={{0,1},{1,0},{2,3},{3,2},{4,5},{5,4},{6,7},{7,6},{8,9},{9,8},{10,11... | collective-permute-start | bytes 1572872 | tf_op jit(solution)/shard_map/ppermute | solution.py:223
  51.9 14.7 %collective-permute-start.6 = (bf16[8,2,32,512]{3,2,1,0:T(8,128)(2,1)S(1)}, bf16[8,2,32,512]{3,2,1,0:T(8,128)(2,1)S(1)}, u32[]{:S(2)}, u32[]{:S(2)}) collective-permute-start(bf16[8,2,32,512]{3,2,1,0:T(8,128)(2,1)S(1)} %collective-permute-done.5.refs_6_), channel_id=1, source_target_pairs={{0,1},{1,0},{2,3},{3,2},{4,5},{5,4},{6,7},{7,6},{8,9},{9,8},{10,11... | collective-permute-start | bytes 1572872 | tf_op jit(solution)/shard_map/ppermute | solution.py:223
  57.2 7.2 %collective-permute-start.17 = (bf16[16,16,512]{2,1,0:T(8,128)(2,1)S(1)}, bf16[16,16,512]{2,1,0:T(8,128)(2,1)S(1)}, u32[]{:S(2)}, u32[]{:S(2)}) collective-permute-start(bf16[16,16,512]{2,1,0:T(8,128)(2,1)S(1)} %pad_maximum_fusion.4), channel_id=1, source_target_pairs={{0,1},{1,0},{2,3},{3,2},{4,5},{5,4},{6,7},{7,6},{8,9},{9,8},{10,11... | collective-permute-start | bytes 786440 | tf_op jit(solution)/shard_map/ppermute | solution.py:223
  64.3 8.0 %collective-permute-start.24 = (bf16[8,2,16,512]{3,2,1,0:T(8,128)(2,1)S(1)}, bf16[8,2,16,512]{3,2,1,0:T(8,128)(2,1)S(1)}, u32[]{:S(2)}, u32[]{:S(2)}) collective-permute-start(bf16[8,2,16,512]{3,2,1,0:T(8,128)(2,1)S(1)} %slice.115), channel_id=1, source_target_pairs={{0,12},{1,13},{2,14},{3,15},{4,0},{5,1},{6,2},{7,3},{8,4},{9,5},{1... | collective-permute-start | bytes 786440 | tf_op jit(solution)/shard_map/ppermute | solution.py:223
  64.6 8.5 %collective-permute-start.26 = (bf16[8,2,16,512]{3,2,1,0:T(8,128)(2,1)S(1)}, bf16[8,2,16,512]{3,2,1,0:T(8,128)(2,1)S(1)}, u32[]{:S(2)}, u32[]{:S(2)}) collective-permute-start(bf16[8,2,16,512]{3,2,1,0:T(8,128)(2,1)S(1)} %slice.116), channel_id=1, source_target_pairs={{0,4},{1,5},{2,6},{3,7},{4,8},{5,9},{6,10},{7,11},{8,12},{9,13},{1... | collective-permute-start | bytes 786440 | tf_op jit(solution)/shard_map/ppermute | solution.py:223
  65.9 14.7 %collective-permute-start.19 = (bf16[8,2,32,512]{3,2,1,0:T(8,128)(2,1)S(1)}, bf16[8,2,32,512]{3,2,1,0:T(8,128)(2,1)S(1)}, u32[]{:S(2)}, u32[]{:S(2)}) collective-permute-start(bf16[8,2,32,512]{3,2,1,0:T(8,128)(2,1)S(1)} %collective-permute-done.18.refs_0_), channel_id=1, source_target_pairs={{0,1},{1,0},{2,3},{3,2},{4,5},{5,4},{6,7},{7,6},{8,9},{9,8},{10,11... | collective-permute-start | bytes 1572872 | tf_op jit(solution)/shard_map/ppermute | solution.py:223
  66.5 14.1 %collective-permute-start.21 = (bf16[8,2,32,512]{3,2,1,0:T(8,128)(2,1)S(1)}, bf16[8,2,32,512]{3,2,1,0:T(8,128)(2,1)S(1)}, u32[]{:S(2)}, u32[]{:S(2)}) collective-permute-start(bf16[8,2,32,512]{3,2,1,0:T(8,128)(2,1)S(1)} %collective-permute-done.20.refs_2_), channel_id=1, source_target_pairs={{0,1},{1,0},{2,3},{3,2},{4,5},{5,4},{6,7},{7,6},{8,9},{9,8},{10,11... | collective-permute-start | bytes 1572872 | tf_op jit(solution)/shard_map/ppermute | solution.py:223
  66.6 14.1 %collective-permute-start.23 = (bf16[8,2,32,512]{3,2,1,0:T(8,128)(2,1)S(1)}, bf16[8,2,32,512]{3,2,1,0:T(8,128)(2,1)S(1)}, u32[]{:S(2)}, u32[]{:S(2)}) collective-permute-start(bf16[8,2,32,512]{3,2,1,0:T(8,128)(2,1)S(1)} %collective-permute-done.22.refs_4_), channel_id=1, source_target_pairs={{0,1},{1,0},{2,3},{3,2},{4,5},{5,4},{6,7},{7,6},{8,9},{9,8},{10,11... | collective-permute-start | bytes 1572872 | tf_op jit(solution)/shard_map/ppermute | solution.py:223
  72.3 15.6 %collective-permute-start.25 = (bf16[8,2,16,512]{3,2,1,0:T(8,128)(2,1)S(1)}, bf16[8,2,16,512]{3,2,1,0:T(8,128)(2,1)S(1)}, u32[]{:S(2)}, u32[]{:S(2)}) collective-permute-start(bf16[8,2,16,512]{3,2,1,0:T(8,128)(2,1)S(1)} %collective-permute-done.24.refs_0_), channel_id=1, source_target_pairs={{0,1},{1,0},{2,3},{3,2},{4,5},{5,4},{6,7},{7,6},{8,9},{9,8},{10,11... | collective-permute-start | bytes 786440 | tf_op jit(solution)/shard_map/ppermute | solution.py:223
  73.1 14.8 %collective-permute-start.27 = (bf16[8,2,16,512]{3,2,1,0:T(8,128)(2,1)S(1)}, bf16[8,2,16,512]{3,2,1,0:T(8,128)(2,1)S(1)}, u32[]{:S(2)}, u32[]{:S(2)}) collective-permute-start(bf16[8,2,16,512]{3,2,1,0:T(8,128)(2,1)S(1)} %collective-permute-done.26.refs_2_), channel_id=1, source_target_pairs={{0,1},{1,0},{2,3},{3,2},{4,5},{5,4},{6,7},{7,6},{8,9},{9,8},{10,11... | collective-permute-start | bytes 786440 | tf_op jit(solution)/shard_map/ppermute | solution.py:223
  (16 other events, 407.8 us)

commit v2 on v1

v2 whole, which is shorter than its diff:
```python
import math

import jax
import jax.numpy as jnp
import numpy as np
from jax import lax
from jax.experimental import pallas as pl
from jax.experimental.pallas import tpu as pltpu
from jax.sharding import PartitionSpec as P

BLOCK = 512
FREQ = 512
LAGS = 256
SEG = 8
SOURCES = 16
HALF = 16
STEP = BLOCK // SOURCES
GROUP = 2 * SEG * HALF
EPS = 1e-06
MIB = 1 << 20

BATCHES = (
    (
        ((0, 0, 0), (0, 0, 1)),
        ((1, 0, 0), (1, 0, 1)),
        ((3, 0, 0), (3, 0, 1)),
        ((0, 1, 0), (0, 1, 1)),
    ),
    (
        ((2, 0, 0), (1, 1, 1)),
        ((3, 1, 0), (2, 0, 1)),
        ((1, 1, 0), (3, 1, 1)),
    ),
    (((2, 1, 1),), ((2, 1, 0),)),
)


def ordered_groups(batch):
    return [(dx, dz, dc, half) for piece in batch for dc in (0, 1) for dx, dz, half in piece]


GROUPS = [group for batch in BATCHES for group in ordered_groups(batch)]

EARLY = sum(len(ordered_groups(batch)) for batch in BATCHES[:2])


def dot(a, b, dims=((1,), (0,))):
    return lax.dot_general(a, b, (dims, ((), ())), preferred_element_type=jnp.float32)


def place(col, dx, dz, dc):
    x, z, core = col // 4, col // 2 % 2, col % 2
    return (x + 4 - dx) % 4 * 4 + (z + dz) % 2 * 2 + (core + dc) % 2


def prepare_kernel(x_ref, mask_ref, src_ref, energy_ref, good_ref):
    mask = mask_ref[...].astype(jnp.float32)
    good_ref[...] = mask
    row = lax.broadcasted_iota(jnp.int32, (SOURCES, BLOCK), 0)
    col = lax.broadcasted_iota(jnp.int32, (SOURCES, BLOCK), 1)
    pick = jnp.where(col == row * STEP, jnp.broadcast_to(mask, (SOURCES, BLOCK)), 0.0).astype(jnp.bfloat16)
    for half in range(2):
        part = x_ref[:, :, half * HALF : (half + 1) * HALF, :].reshape(GROUP, BLOCK)
        src_ref[:, half * GROUP : (half + 1) * GROUP] = dot(pick, part, ((1,), (1,))).astype(jnp.bfloat16)
    sums = []
    for seg in range(SEG):
        value = x_ref[seg].astype(jnp.float32).reshape(4 * HALF, BLOCK)
        sums.append(jnp.sum(value * value, axis=0, keepdims=True))
    energy = jnp.concatenate(sums, axis=0) * mask
    high = energy.astype(jnp.bfloat16).astype(jnp.float32)
    energy_ref[...] = jnp.concatenate([high, energy - high], axis=0).astype(jnp.bfloat16)


def prepare(x, mask):
    return pl.pallas_call(
        prepare_kernel,
        out_shape=(jax.ShapeDtypeStruct((SOURCES, BLOCK), jnp.bfloat16),) * 2
        + (jax.ShapeDtypeStruct((1, BLOCK), jnp.float32),),
        compiler_params=pltpu.CompilerParams(vmem_limit_bytes=16 * MIB),
    )(x, mask)


def choose_kernel(row_ref, pairing_ref, gathered_ref, energy_ref, out_ref):
    row = row_ref[0]
    for slot in range(16):
        block = pairing_ref[0, slot]
        out_ref[slot, :SOURCES] = gathered_ref[block % 4, (row // 4 + 4 - block // 4) % 4]
        out_ref[slot, SOURCES:] = energy_ref[...]


def choose(row, pairing, gathered, energy):
    return pl.pallas_call(
        choose_kernel,
        out_shape=jax.ShapeDtypeStruct((16, 2 * SOURCES, BLOCK), jnp.bfloat16),
        in_specs=[pl.BlockSpec(memory_space=pltpu.SMEM)] * 2 + [pl.BlockSpec(memory_space=pltpu.VMEM)] * 2,
        compiler_params=pltpu.CompilerParams(vmem_limit_bytes=8 * MIB),
    )(row, pairing, gathered, energy)


def scales_kernel(col_ref, got_ref, good_ref, scale_ref, white_ref):
    energy = jnp.zeros((SEG, BLOCK), jnp.float32)
    for n in range(16):
        both = got_ref[n, SOURCES:].astype(jnp.float32)
        energy = energy + (both[:SEG] + both[SEG:])
    scale_ref[...] = good_ref[...] * lax.rsqrt(energy / FREQ + EPS)

    power = jnp.zeros((SOURCES, 2 * GROUP), jnp.float32)
    for n in range(16):
        value = got_ref[n, :SOURCES].astype(jnp.float32)
        power = power + value * value
    power = power[:, :GROUP] + power[:, GROUP:]
    row = lax.broadcasted_iota(jnp.int32, (GROUP, GROUP), 0)
    col = lax.broadcasted_iota(jnp.int32, (GROUP, GROUP), 1)
    same = jnp.where(row // (2 * HALF) == col // (2 * HALF), 1.0, 0.0)
    total = lax.dot_general(
        power, same, (((1,), (0,)), ((), ())), precision=lax.Precision.HIGHEST, preferred_element_type=jnp.float32
    )
    factor = lax.rsqrt(total / FREQ + EPS)
    turn = jnp.where(row == col + HALF, 1.0, 0.0) - jnp.where(row == col - HALF, 1.0, 0.0)
    first = (col // HALF) % 2 == 0
    turn = jnp.where(first, jnp.maximum(turn, 0.0), jnp.minimum(turn, 0.0)).astype(jnp.bfloat16)
    for g, (dx, dz, dc, half) in enumerate(GROUPS):
        n = place(col_ref[0], dx, dz, dc)
        value = got_ref[n, :SOURCES, half * GROUP : (half + 1) * GROUP].astype(jnp.float32)
        real = (value * factor).astype(jnp.bfloat16)
        white_ref[g, :SOURCES] = real
        white_ref[g, SOURCES:] = dot(real, turn).astype(jnp.bfloat16)


def scales(col, got, good):
    return pl.pallas_call(
        scales_kernel,
        out_shape=(
            jax.ShapeDtypeStruct((SEG, BLOCK), jnp.float32),
            jax.ShapeDtypeStruct((len(GROUPS), 2 * SOURCES, GROUP), jnp.bfloat16),
        ),
        in_specs=[pl.BlockSpec(memory_space=pltpu.SMEM)] + [pl.BlockSpec(memory_space=pltpu.VMEM)] * 2,
        compiler_params=pltpu.CompilerParams(vmem_limit_bytes=8 * MIB),
    )(col, got, good)


def cross_groups(pieces, first_group, scale_ref, white_ref, crossed, raw, right0, right1, left0, left1, sems):
    copies = []
    for piece in pieces:
        for half in range(piece.shape[2] // HALF):
            g = len(copies)
            copies.append(pltpu.make_async_copy(piece.at[:, :, pl.ds(half * HALF, HALF), :], raw.at[g], sems.at[g]))
    for copy in copies:
        copy.start()
    groups = len(copies)

    def arrive(g):
        pltpu.make_async_copy(raw.at[g], raw.at[g], sems.at[g]).wait()

    lane = lax.broadcasted_iota(jnp.int32, (HALF, GROUP), 1)
    sub = lax.broadcasted_iota(jnp.int32, (HALF, GROUP), 0)
    diagonal = lane % HALF == sub

    def ready(g, right, left):
        for seg in range(SEG):
            value = raw[g, seg].astype(jnp.float32) * scale_ref[seg : seg + 1, :].reshape(1, 1, BLOCK)
            right[seg * 2 * HALF : (seg + 1) * 2 * HALF, :] = value.astype(jnp.bfloat16).reshape(2 * HALF, BLOCK)
        white = white_ref[first_group + g].astype(jnp.float32)
        for v in range(SOURCES):
            for part in range(2):
                one = white[part * SOURCES + v : part * SOURCES + v + 1, :]
                tile = jnp.where(diagonal, jnp.broadcast_to(one, (HALF, GROUP)), 0.0).astype(jnp.bfloat16)
                left[(2 * v + part) * HALF : (2 * v + part + 1) * HALF, :] = tile

    def multiply(g, right, left):
        rows = pl.ds(pl.multiple_of(g * 2 * HALF, 2 * HALF), 2 * HALF)
        for n in range(0, BLOCK, GROUP):
            value = dot(left[...], right[:, n : n + GROUP]).astype(jnp.bfloat16)
            crossed[:, rows, n : n + GROUP] = value.reshape(SOURCES, 2 * HALF, GROUP)

    arrive(0)
    ready(0, right0, left0)

    def pair(i, carry):
        g = 2 * i
        arrive(g + 1)
        multiply(g, right0, left0)
        ready(g + 1, right1, left1)

        @pl.when(i < groups // 2 - 1)
        def _():
            arrive(g + 2)

        multiply(g + 1, right1, left1)
        ready(jnp.minimum(g + 2, groups - 1), right0, left0)
        return carry

    lax.fori_loop(0, groups // 2, pair, 0)


def cross_scratch(groups):
    return [
        pltpu.VMEM((groups, SEG, 2, HALF, BLOCK), jnp.bfloat16),
        pltpu.VMEM((GROUP, BLOCK), jnp.bfloat16),
        pltpu.VMEM((GROUP, BLOCK), jnp.bfloat16),
        pltpu.VMEM((2 * SOURCES * HALF, GROUP), jnp.bfloat16),
        pltpu.VMEM((2 * SOURCES * HALF, GROUP), jnp.bfloat16),
        pltpu.SemaphoreType.DMA((groups,)),
    ]


def cross(pieces, scale, white):
    def kernel(*refs):
        scale_ref, white_ref, out_ref = refs[len(pieces) : len(pieces) + 3]
        cross_groups(refs[: len(pieces)], 0, scale_ref, white_ref, out_ref, *refs[len(pieces) + 3 :])

    return pl.pallas_call(
        kernel,
        out_shape=jax.ShapeDtypeStruct((SOURCES, EARLY * 2 * HALF, BLOCK), jnp.bfloat16),
        in_specs=[pl.BlockSpec(memory_space=pl.ANY)] * len(pieces) + [pl.BlockSpec(memory_space=pltpu.VMEM)] * 2,
        scratch_shapes=cross_scratch(EARLY),
        compiler_params=pltpu.CompilerParams(vmem_limit_bytes=28 * MIB),
        cost_estimate=pl.CostEstimate(flops=10**9, bytes_accessed=MIB, transcendentals=0),
    )(*pieces, scale, white)


def finish(pieces, early, scale, white, table):
    count, late = len(pieces), len(GROUPS) - EARLY

    def kernel(*refs):
        early_ref, scale_ref, white_ref, table_ref, out_ref, crossed, staged0, staged1, out_sems = refs[count : count + 9]
        cross_groups(refs[:count], EARLY, scale_ref, white_ref, crossed, *refs[count + 9 :])
        split = EARLY * 2 * HALF

        def result(v, staged, slot):
            return pltpu.make_async_copy(staged, out_ref.at[v], out_sems.at[slot])

        def lags(i, carry):
            for slot, staged in ((0, staged0), (1, staged1)):
                v = 2 * i + slot

                @pl.when(i > 0)
                def _():
                    result(v - 2, staged, slot).wait()

                total = dot(table_ref[:, :split], early_ref[v]) + dot(table_ref[:, split:], crossed[v])
                staged[...] = total.astype(jnp.bfloat16)
                result(v, staged, slot).start()
            return carry

        lax.fori_loop(0, SOURCES // 2, lags, 0)
        result(SOURCES - 2, staged0, 0).wait()
        result(SOURCES - 1, staged1, 1).wait()

    return pl.pallas_call(
        kernel,
        out_shape=jax.ShapeDtypeStruct((SOURCES, LAGS, BLOCK), jnp.bfloat16),
        in_specs=[pl.BlockSpec(memory_space=pl.ANY)] * count + [pl.BlockSpec(memory_space=pltpu.VMEM)] * 4,
        out_specs=pl.BlockSpec(memory_space=pl.ANY),
        scratch_shapes=[
            pltpu.VMEM((SOURCES, late * 2 * HALF, BLOCK), jnp.bfloat16),
            pltpu.VMEM((LAGS, BLOCK), jnp.bfloat16),
            pltpu.VMEM((LAGS, BLOCK), jnp.bfloat16),
            pltpu.SemaphoreType.DMA((2,)),
            *cross_scratch(late),
        ],
        compiler_params=pltpu.CompilerParams(vmem_limit_bytes=26 * MIB),
        cost_estimate=pl.CostEstimate(flops=5 * 10**9, bytes_accessed=5 * MIB, transcendentals=0),
    )(*pieces, early, scale, white, table)


def table_kernel(col_ref, out_ref):
    col = col_ref[0]
    lane = lax.broadcasted_iota(jnp.int32, (1, 2 * FREQ), 1)
    freq = lane % HALF
    for g, (dx, dz, dc, half) in enumerate(GROUPS):
        base = place(col, dx, dz, dc) * 2 * HALF + half * HALF
        freq = freq + jnp.where(lane // (2 * HALF) == g, base, 0)
    shift = lane // HALF % 2 * (FREQ // 2)
    step = lax.broadcasted_iota(jnp.int32, (HALF, 2 * FREQ), 0)
    cosine = lambda phase: jnp.cos((phase % (2 * FREQ)).astype(jnp.float32) * (math.pi / FREQ))
    coarse, fine = HALF * step * freq + shift, step * freq
    quarter = 3 * FREQ // 2
    weight = jnp.where(freq == 0, 0.5, 1.0).astype(jnp.float32) / math.sqrt(2.0 * FREQ)
    cos0, sin0 = weight * cosine(coarse), weight * cosine(coarse + quarter)
    cos1, sin1 = cosine(fine), cosine(fine + quarter)
    for i in range(HALF):
        value = cos0[i : i + 1] * cos1 - sin0[i : i + 1] * sin1
        out_ref[i * HALF : (i + 1) * HALF, :] = value.astype(jnp.bfloat16)


def lag_table(col):
    return pl.pallas_call(
        table_kernel,
        out_shape=jax.ShapeDtypeStruct((LAGS, 2 * FREQ), jnp.bfloat16),
        in_specs=[pl.BlockSpec(memory_space=pltpu.SMEM)],
        compiler_params=pltpu.CompilerParams(vmem_limit_bytes=8 * MIB),
        cost_estimate=pl.CostEstimate(flops=10**6, bytes_accessed=10**4, transcendentals=0),
    )(col)


def send(value, axis, where):
    return lax.ppermute(value, axis, [(n, where(n)) for n in range(16)])


def on_slow(n, d):
    return (n // 4 + d) % 4 * 4 + n % 4


def spread(value, axis, groups):
    copies = jnp.broadcast_to(value[None], (len(groups[0]), *value.shape))
    return lax.all_to_all(copies, axis, 0, 0, tiled=True, axis_index_groups=groups)


def on_device(x, mask, pairing):
    col = lax.axis_index("col")
    up = lambda v: send(v, "col", lambda n: on_slow(n, 1))
    down = lambda v: send(v, "col", lambda n: on_slow(n, -1))
    across = lambda v: send(v, "col", lambda n: n ^ 2)
    sibling = lambda v: send(v, "col", lambda n: n ^ 1)
    low = lambda v: v[:, :, :HALF]
    high = lambda v: v[:, :, HALF:]
    join = lambda a, b: jnp.concatenate([a, b], axis=2)

    a1, b1, c1 = up(x), down(x), across(x)

    own, partial, good = prepare(x, mask.reshape(1, BLOCK))
    by_slow = jnp.stack([own] + [send(own, "row", lambda n, d=d: on_slow(n, d)) for d in (1, 2, 3)])
    by_row = spread(by_slow, "row", [[4 * a + b for b in range(4)] for a in range(4)])
    a2, b2, c2 = up(join(low(a1), high(c1))), down(join(low(c1), high(b1))), across(join(low(a1), high(b1)))
    a3, b3 = up(high(a2)), down(low(b2))
    chosen = choose(lax.axis_index("row").reshape(1), pairing, by_row, partial)
    chosen, table = lax.optimization_barrier((chosen, lag_table(col.reshape(1))))
    got = lax.all_to_all(chosen, "col", 0, 0, tiled=True)
    scale, white = scales(col.reshape(1), got, good)

    pair = lambda *mine: [piece for one in mine for piece in (one, sibling(one))]
    early = cross(pair(x, a1, b1, c1, a2, b2, c2), scale, white)
    early, a3, b3 = lax.optimization_barrier((early, a3, b3))
    return finish(pair(a3, b3), early, scale, white, table)


def solution(mesh):
    in_specs = (P(None, None, "col", "row"), P("row"), P("row", None))
    out_specs = P("col", None, "row")
    return jax.shard_map(on_device, mesh=mesh, in_specs=in_specs, out_specs=out_specs, check_vma=False)
```

time: 103 us -> 84.3 us (0.82)
  the two profiles are of different devices: /device:TPU:1 before, /device:TPU:17 now
where the time goes in v2:
time: 84.3 us; the launch traced here: 83.8 us
  starting transfers between devices  40.9 us (49%)
  Pallas kernels  27.7 us (33%)
  local copies, waits for them, and re-layouts  8.21 us (10%)
  waiting for transfers between devices  5.44 us (6%)
  other arithmetic  1.24 us (1%)
    ppermute x20, starting transfers between devices, send(): return lax.ppermute(value, axis, [(n, where(n)) for n in range(16)])  31.9 us
    pallas_call x1, Pallas kernels, finish(): pl.pallas_call(kernel, out_shape=jax.ShapeDtypeStruct((SOURCES, LAGS, BLO...  12 us
    pallas_call x1, Pallas kernels, cross(): pl.pallas_call(kernel, out_shape=jax.ShapeDtypeStruct((SOURCES, EARLY * 2...  10.6 us
    ppermute x20, waiting for transfers between devices, send(): return lax.ppermute(value, axis, [(n, where(n)) for n in range(16)])  5.43 us
    unnamed x12, local copies, waits for them, and re-layouts  5.01 us
    all_to_all x1, starting transfers between devices, on_device(): got = lax.all_to_all(chosen, 'col', 0, 0, tiled=True)  4.75 us
    all_to_all x1, starting transfers between devices, spread(): lax.all_to_all(copies, axis, 0, 0, tiled=True, axis_index_groups=groups)  4.24 us
    slice x2, local copies, waits for them, and re-layouts, on_device(): high = lambda v: v[:, :, HALF:]  1.69 us
  transfers between devices with their start and end apart: 22, of which 4 were waited for; matrix products, arithmetic and copies ran while one was open for 5% of the time, Pallas kernels for 19%

profile of v2, /device:TPU:17, one launch (start us, length us, event | category | flops | bytes accessed | tf_op | source)
XLA Modules:
  0.0 83.8 jit_solution(10768075911928097641)
XLA Ops:
  0.0 1.2 %collective-permute-start.1 = (bf16[8,2,32,512]{3,2,1,0:T(8,128)(2,1)}, bf16[8,2,32,512]{3,2,1,0:T(8,128)(2,1)S(1)}, u32[]{:S(2)}, u32[]{:S(2)}) collective-permute-start(bf16[8,2,32,512]{3,2,1,0:T(8,128)(2,1)} %refs_0_.1), channel_id=1, source_target_pairs={{0,4},{1,5},{2,6},{3,7},{4,8},{5,9},{6,10},{7,11},{8,12},{9,13},{1... | collective-permute-start | bytes 1572872 | tf_op jit(solution)/shard_map/ppermute | solution.py:298
  1.2 1.6 %collective-permute-start.5 = (bf16[8,2,32,512]{3,2,1,0:T(8,128)(2,1)}, bf16[8,2,32,512]{3,2,1,0:T(8,128)(2,1)S(1)}, u32[]{:S(2)}, u32[]{:S(2)}) collective-permute-start(bf16[8,2,32,512]{3,2,1,0:T(8,128)(2,1)} %refs_0_.1), channel_id=1, source_target_pairs={{0,2},{1,3},{2,0},{3,1},{4,6},{5,7},{6,4},{7,5},{8,10},{9,11},{10,... | collective-permute-start | bytes 1572872 | tf_op jit(solution)/shard_map/ppermute | solution.py:298
  2.9 1.5 %collective-permute-start.3 = (bf16[8,2,32,512]{3,2,1,0:T(8,128)(2,1)}, bf16[8,2,32,512]{3,2,1,0:T(8,128)(2,1)S(1)}, u32[]{:S(2)}, u32[]{:S(2)}) collective-permute-start(bf16[8,2,32,512]{3,2,1,0:T(8,128)(2,1)} %refs_0_.1), channel_id=1, source_target_pairs={{0,12},{1,13},{2,14},{3,15},{4,0},{5,1},{6,2},{7,3},{8,4},{9,5},{1... | collective-permute-start | bytes 1572872 | tf_op jit(solution)/shard_map/ppermute | solution.py:298
  5.0 1.3 %shard_map.37 = (bf16[16,512]{1,0:T(8,128)(2,1)S(1)}, bf16[16,512]{1,0:T(8,128)(2,1)S(1)}, f32[1,512]{1,0:T(1,128)S(1)}) custom-call(bf16[8,2,32,512]{3,2,1,0:T(8,128)(2,1)} %refs_0_.1, s32[1,512]{1,0:T(1,128)S(1)} %bitcast.8), custom_call_target="tpu_custom_call" | custom-call | tf_op jit(solution)/shard_map/pallas_call | solution.py:75
  6.3 3.0 %collective-permute-start.13 = (bf16[16,512]{1,0:T(8,128)(2,1)S(1)}, bf16[16,512]{1,0:T(8,128)(2,1)S(1)}, u32[]{:S(2)}, u32[]{:S(2)}) collective-permute-start(bf16[16,512]{1,0:T(8,128)(2,1)S(1)} %get-tuple-element.15), channel_id=1, source_target_pairs={{0,64},{16,80},{32,96},{48,112},{64,128},{80,144},{96,160},{112,17... | collective-permute-start | bytes 49160 | tf_op jit(solution)/shard_map/ppermute | solution.py:298
  9.3 4.2 %collective-permute-start.14 = (bf16[16,512]{1,0:T(8,128)(2,1)S(1)}, bf16[16,512]{1,0:T(8,128)(2,1)S(1)}, u32[]{:S(2)}, u32[]{:S(2)}) collective-permute-start(bf16[16,512]{1,0:T(8,128)(2,1)S(1)} %get-tuple-element.15), channel_id=1, source_target_pairs={{0,128},{16,144},{32,160},{48,176},{64,192},{80,208},{96,224},{112... | collective-permute-start | bytes 49160 | tf_op jit(solution)/shard_map/ppermute | solution.py:298
  14.2 6.0 %collective-permute-start.15 = (bf16[16,512]{1,0:T(8,128)(2,1)S(1)}, bf16[16,512]{1,0:T(8,128)(2,1)S(1)}, u32[]{:S(2)}, u32[]{:S(2)}) collective-permute-start(bf16[16,512]{1,0:T(8,128)(2,1)S(1)} %get-tuple-element.15), channel_id=1, source_target_pairs={{0,192},{16,208},{32,224},{48,240},{64,0},{80,16},{96,32},{112,48}... | collective-permute-start | bytes 49160 | tf_op jit(solution)/shard_map/ppermute | solution.py:298
  20.3 1.9 %collective-permute-start = (bf16[8,2,32,512]{3,2,1,0:T(8,128)(2,1)}, bf16[8,2,32,512]{3,2,1,0:T(8,128)(2,1)}, u32[]{:S(2)}, u32[]{:S(2)}) collective-permute-start(bf16[8,2,32,512]{3,2,1,0:T(8,128)(2,1)} %refs_0_.1), channel_id=1, source_target_pairs={{0,1},{1,0},{2,3},{3,2},{4,5},{5,4},{6,7},{7,6},{8,9},{9,8},{10,11... | collective-permute-start | bytes 1572872 | tf_op jit(solution)/shard_map/ppermute | solution.py:298
  22.3 1.2 %pad_maximum_fusion = (bf16[8,2,32,512]{3,2,1,0:T(8,128)(2,1)}, bf16[8,2,32,512]{3,2,1,0:T(8,128)(2,1)}, bf16[8,2,32,512]{3,2,1,0:T(8,128)(2,1)}) fusion(bf16[8,2,16,512]{3,2,1,0:T(8,128)(2,1)S(1)} %slice.26, bf16[8,2,16,512]{3,2,1,0:T(8,128)(2,1)S(1)} %slice.29, bf16[8,2,16,512]{3,2,1,0:T(8,128)(2,1)S(1)} %get-tuple-element.25, ...), kind=kLoop, calls=%fused_computation | loop fusion | flops 2621440 | bytes 2621440 | tf_op jit(solution)/shard_map/concatenate | solution.py:318
  23.5 1.3 %collective-permute-start.9 = (bf16[8,2,32,512]{3,2,1,0:T(8,128)(2,1)}, bf16[8,2,32,512]{3,2,1,0:T(8,128)(2,1)S(1)}, u32[]{:S(2)}, u32[]{:S(2)}) collective-permute-start(bf16[8,2,32,512]{3,2,1,0:T(8,128)(2,1)} %get-tuple-element.28), channel_id=1, source_target_pairs={{0,12},{1,13},{2,14},{3,15},{4,0},{5,1},{6,2},{7,3},{8,4},{9,5},{1... | collective-permute-start | bytes 1572872 | tf_op jit(solution)/shard_map/ppermute | solution.py:298
  25.5 4.2 %all-to-all-start = ((bf16[4,4,16,512]{3,2,1,0:T(8,128)(2,1)}), bf16[4,4,16,512]{3,2,1,0:T(8,128)(2,1)S(1)}, u32[]{:S(2)}, u32[]{:S(2)}) async-start(bf16[4,4,16,512]{3,2,1,0:T(8,128)(2,1)} %broadcast_in_dim.2), calls=%async_computation | async-start | bytes 524288 | tf_op jit(solution)/shard_map/all_to_all | solution.py:307
  30.7 1.4 %collective-permute-start.2 = (bf16[8,2,32,512]{3,2,1,0:T(8,128)(2,1)S(1)}, bf16[8,2,32,512]{3,2,1,0:T(8,128)(2,1)}, u32[]{:S(2)}, u32[]{:S(2)}) collective-permute-start(bf16[8,2,32,512]{3,2,1,0:T(8,128)(2,1)S(1)} %collective-permute-done.1.refs_2_), channel_id=1, source_target_pairs={{0,1},{1,0},{2,3},{3,2},{4,5},{5,4},{6,7},{7,6},{8,9},{9,8},{10,11... | collective-permute-start | bytes 1572872 | tf_op jit(solution)/shard_map/ppermute | solution.py:298
  32.1 1.2 %shard_map.39.refs_7_ = bf16[256,1024]{1,0:T(8,128)(2,1)S(1)} custom-call(s32[1]{0:T(128)} %bitcast.col_ref), custom_call_target="tpu_custom_call" | custom-call | flops 1000000 | bytes 10000 | tf_op jit(solution)/shard_map/pallas_call | solution.py:288
  34.0 1.5 %shard_map.38 = bf16[16,32,512]{2,1,0:T(8,128)(2,1)} custom-call(s32[1]{0:T(128)} %bitcast.1.row_ref, s32[1,16]{1,0:T(1,128)S(1)} %copy-done.5, bf16[4,4,16,512]{3,2,1,0:T(8,128)(2,1)S(1)} %all-to-all-done.gathered_ref, bf16[16,512]{1,0:T(8,128)(2,1)S(1)} %get-tuple-element.16.energy_ref), custom_call_target="tpu_custom_call" | custom-call | tf_op jit(solution)/shard_map/pallas_call | solution.py:92
  35.5 4.7 %all-to-all-start.1 = ((bf16[16,32,512]{2,1,0:T(8,128)(2,1)}), bf16[16,32,512]{2,1,0:T(8,128)(2,1)S(1)}, u32[]{:S(2)}, u32[]{:S(2)}) async-start(bf16[16,32,512]{2,1,0:T(8,128)(2,1)} %shard_map.38), calls=%async_computation.1 | async-start | bytes 1048576 | tf_op jit(solution)/shard_map/all_to_all | solution.py:329
  40.8 3.0 %collective-permute-done.7.refs_8_ = bf16[8,2,32,512]{3,2,1,0:T(8,128)(2,1)} collective-permute-done((bf16[8,2,32,512]{3,2,1,0:T(8,128)(2,1)}, bf16[8,2,32,512]{3,2,1,0:T(8,128)(2,1)}, u32[]{:S(2)}, u32[]{:S(2)}) %collective-permute-start.7) | collective-permute-done | bytes 524320 | tf_op jit(solution)/shard_map/ppermute | solution.py:298
  43.8 4.0 %collective-permute-start.10 = (bf16[8,2,32,512]{3,2,1,0:T(8,128)(2,1)S(1)}, bf16[8,2,32,512]{3,2,1,0:T(8,128)(2,1)}, u32[]{:S(2)}, u32[]{:S(2)}) collective-permute-start(bf16[8,2,32,512]{3,2,1,0:T(8,128)(2,1)S(1)} %collective-permute-done.9.refs_10_), channel_id=1, source_target_pairs={{0,1},{1,0},{2,3},{3,2},{4,5},{5,4},{6,7},{7,6},{8,9},{9,8},{10,11... | collective-permute-start | bytes 1572872 | tf_op jit(solution)/shard_map/ppermute | solution.py:298
  48.4 1.7 %slice.30 = bf16[8,2,16,512]{3,2,1,0:T(8,128)(2,1)} slice(bf16[8,2,32,512]{3,2,1,0:T(8,128)(2,1)} %collective-permute-done.7.refs_8_), slice={[0:8], [0:2], [16:32], [0:512]} | slice | bytes 524288 | tf_op jit(solution)/shard_map/slice | solution.py:317
  52.4 2.7 %collective-permute-start.17 = (bf16[8,2,16,512]{3,2,1,0:T(8,128)(2,1)}, bf16[8,2,16,512]{3,2,1,0:T(8,128)(2,1)}, u32[]{:S(2)}, u32[]{:S(2)}) collective-permute-start(bf16[8,2,16,512]{3,2,1,0:T(8,128)(2,1)} %slice.31), channel_id=1, source_target_pairs={{0,12},{1,13},{2,14},{3,15},{4,0},{5,1},{6,2},{7,3},{8,4},{9,5},{1... | collective-permute-start | bytes 786440 | tf_op jit(solution)/shard_map/ppermute | solution.py:298
  55.1 1.1 %shard_map.40 = (f32[8,512]{1,0:T(8,128)S(1)}, bf16[32,32,256]{2,1,0:T(8,128)(2,1)S(1)}) custom-call(s32[1]{0:T(128)} %bitcast.col_ref, bf16[16,32,512]{2,1,0:T(8,128)(2,1)S(1)} %all-to-all-done.1.got_ref, f32[1,512]{1,0:T(1,128)S(1)} %get-tuple-element.18.good_ref), custom_call_target="tpu_custom_call" | custom-call | tf_op jit(solution)/shard_map/pallas_call | solution.py:131
  57.3 1.0 %copy-done.3 = bf16[8,2,32,512]{3,2,1,0:T(8,128)(2,1)S(1)} copy-done((bf16[8,2,32,512]{3,2,1,0:T(8,128)(2,1)S(1)}, bf16[8,2,32,512]{3,2,1,0:T(8,128)(2,1)}, u32[]{:S(2)}) %copy-start.3) | copy-done | bytes 524312
  58.4 10.6 %shard_map.41.refs_4_ = bf16[16,896,512]{2,1,0:T(8,128)(2,1)S(1)} custom-call(bf16[8,2,32,512]{3,2,1,0:T(8,128)(2,1)} %refs_0_.1, bf16[8,2,32,512]{3,2,1,0:T(8,128)(2,1)} %collective-permute-done.refs_1_, bf16[8,2,32,512]{3,2,1,0:T(8,128)(2,1)S(1)} %collective-permute-done.1.refs_2_, bf16[8,2,32,512]{3,2,1,0:T(8,128)(2,1)} %collective-permute-done.2.refs_3_, ...), custom_call_target="tpu_custom_call" | custom-call | flops 1000000000 | bytes 1048576 | tf_op jit(solution)/shard_map/pallas_call | solution.py:212
  70.0 1.1 %collective-permute-done.18.refs_1_ = bf16[8,2,16,512]{3,2,1,0:T(8,128)(2,1)S(1)} collective-permute-done((bf16[8,2,16,512]{3,2,1,0:T(8,128)(2,1)S(1)}, bf16[8,2,16,512]{3,2,1,0:T(8,128)(2,1)S(1)}, u32[]{:S(2)}, u32[]{:S(2)}) %collective-permute-start.18) | collective-permute-done | bytes 262176 | tf_op jit(solution)/shard_map/ppermute | solution.py:298
  71.6 12.0 %shard_map.42 = bf16[16,256,512]{2,1,0:T(8,128)(2,1)} custom-call(bf16[8,2,16,512]{3,2,1,0:T(8,128)(2,1)S(1)} %collective-permute-done.16.refs_0_, bf16[8,2,16,512]{3,2,1,0:T(8,128)(2,1)S(1)} %collective-permute-done.18.refs_1_, bf16[8,2,16,512]{3,2,1,0:T(8,128)(2,1)} %collective-permute-done.17.refs_2_, ...), custom_call_target="tpu_custom_call" | custom-call | flops 5000000000 | bytes 5242880 | tf_op jit(solution)/shard_map/pallas_call | solution.py:250
  (46 shorter events, 9.9 us)
Async XLA Ops:
  0.0 14.2 %collective-permute-start.1 = (bf16[8,2,32,512]{3,2,1,0:T(8,128)(2,1)}, bf16[8,2,32,512]{3,2,1,0:T(8,128)(2,1)S(1)}, u32[]{:S(2)}, u32[]{:S(2)}) collective-permute-start(bf16[8,2,32,512]{3,2,1,0:T(8,128)(2,1)} %refs_0_.1), channel_id=1, source_target_pairs={{0,4},{1,5},{2,6},{3,7},{4,8},{5,9},{6,10},{7,11},{8,12},{9,13},{1... | collective-permute-start | bytes 1572872 | tf_op jit(solution)/shard_map/ppermute | solution.py:298
  1.2 19.0 %collective-permute-start.5 = (bf16[8,2,32,512]{3,2,1,0:T(8,128)(2,1)}, bf16[8,2,32,512]{3,2,1,0:T(8,128)(2,1)S(1)}, u32[]{:S(2)}, u32[]{:S(2)}) collective-permute-start(bf16[8,2,32,512]{3,2,1,0:T(8,128)(2,1)} %refs_0_.1), channel_id=1, source_target_pairs={{0,2},{1,3},{2,0},{3,1},{4,6},{5,7},{6,4},{7,5},{8,10},{9,11},{10,... | collective-permute-start | bytes 1572872 | tf_op jit(solution)/shard_map/ppermute | solution.py:298
  2.9 19.4 %collective-permute-start.3 = (bf16[8,2,32,512]{3,2,1,0:T(8,128)(2,1)}, bf16[8,2,32,512]{3,2,1,0:T(8,128)(2,1)S(1)}, u32[]{:S(2)}, u32[]{:S(2)}) collective-permute-start(bf16[8,2,32,512]{3,2,1,0:T(8,128)(2,1)} %refs_0_.1), channel_id=1, source_target_pairs={{0,12},{1,13},{2,14},{3,15},{4,0},{5,1},{6,2},{7,3},{8,4},{9,5},{1... | collective-permute-start | bytes 1572872 | tf_op jit(solution)/shard_map/ppermute | solution.py:298
  6.3 18.5 %collective-permute-start.13 = (bf16[16,512]{1,0:T(8,128)(2,1)S(1)}, bf16[16,512]{1,0:T(8,128)(2,1)S(1)}, u32[]{:S(2)}, u32[]{:S(2)}) collective-permute-start(bf16[16,512]{1,0:T(8,128)(2,1)S(1)} %get-tuple-element.15), channel_id=1, source_target_pairs={{0,64},{16,80},{32,96},{48,112},{64,128},{80,144},{96,160},{112,17... | collective-permute-start | bytes 49160 | tf_op jit(solution)/shard_map/ppermute | solution.py:298
  9.3 15.5 %collective-permute-start.14 = (bf16[16,512]{1,0:T(8,128)(2,1)S(1)}, bf16[16,512]{1,0:T(8,128)(2,1)S(1)}, u32[]{:S(2)}, u32[]{:S(2)}) collective-permute-start(bf16[16,512]{1,0:T(8,128)(2,1)S(1)} %get-tuple-element.15), channel_id=1, source_target_pairs={{0,128},{16,144},{32,160},{48,176},{64,192},{80,208},{96,224},{112... | collective-permute-start | bytes 49160 | tf_op jit(solution)/shard_map/ppermute | solution.py:298
  14.2 10.5 %collective-permute-start.15 = (bf16[16,512]{1,0:T(8,128)(2,1)S(1)}, bf16[16,512]{1,0:T(8,128)(2,1)S(1)}, u32[]{:S(2)}, u32[]{:S(2)}) collective-permute-start(bf16[16,512]{1,0:T(8,128)(2,1)S(1)} %get-tuple-element.15), channel_id=1, source_target_pairs={{0,192},{16,208},{32,224},{48,240},{64,0},{80,16},{96,32},{112,48}... | collective-permute-start | bytes 49160 | tf_op jit(solution)/shard_map/ppermute | solution.py:298
  20.3 19.9 %collective-permute-start = (bf16[8,2,32,512]{3,2,1,0:T(8,128)(2,1)}, bf16[8,2,32,512]{3,2,1,0:T(8,128)(2,1)}, u32[]{:S(2)}, u32[]{:S(2)}) collective-permute-start(bf16[8,2,32,512]{3,2,1,0:T(8,128)(2,1)} %refs_0_.1), channel_id=1, source_target_pairs={{0,1},{1,0},{2,3},{3,2},{4,5},{5,4},{6,7},{7,6},{8,9},{9,8},{10,11... | collective-permute-start | bytes 1572872 | tf_op jit(solution)/shard_map/ppermute | solution.py:298
  23.5 17.0 %collective-permute-start.9 = (bf16[8,2,32,512]{3,2,1,0:T(8,128)(2,1)}, bf16[8,2,32,512]{3,2,1,0:T(8,128)(2,1)S(1)}, u32[]{:S(2)}, u32[]{:S(2)}) collective-permute-start(bf16[8,2,32,512]{3,2,1,0:T(8,128)(2,1)} %get-tuple-element.28), channel_id=1, source_target_pairs={{0,12},{1,13},{2,14},{3,15},{4,0},{5,1},{6,2},{7,3},{8,4},{9,5},{1... | collective-permute-start | bytes 1572872 | tf_op jit(solution)/shard_map/ppermute | solution.py:298
  25.5 7.8 %all-to-all-start = ((bf16[4,4,16,512]{3,2,1,0:T(8,128)(2,1)}), bf16[4,4,16,512]{3,2,1,0:T(8,128)(2,1)S(1)}, u32[]{:S(2)}, u32[]{:S(2)}) async-start(bf16[4,4,16,512]{3,2,1,0:T(8,128)(2,1)} %broadcast_in_dim.2), calls=%async_computation | async-start | bytes 524288 | tf_op jit(solution)/shard_map/all_to_all | solution.py:307
  29.7 14.1 %collective-permute-start.7 = (bf16[8,2,32,512]{3,2,1,0:T(8,128)(2,1)}, bf16[8,2,32,512]{3,2,1,0:T(8,128)(2,1)}, u32[]{:S(2)}, u32[]{:S(2)}) collective-permute-start(bf16[8,2,32,512]{3,2,1,0:T(8,128)(2,1)} %get-tuple-element.29), channel_id=1, source_target_pairs={{0,4},{1,5},{2,6},{3,7},{4,8},{5,9},{6,10},{7,11},{8,12},{9,13},{1... | collective-permute-start | bytes 1572872 | tf_op jit(solution)/shard_map/ppermute | solution.py:298
  29.9 17.9 %collective-permute-start.11 = (bf16[8,2,32,512]{3,2,1,0:T(8,128)(2,1)}, bf16[8,2,32,512]{3,2,1,0:T(8,128)(2,1)}, u32[]{:S(2)}, u32[]{:S(2)}) collective-permute-start(bf16[8,2,32,512]{3,2,1,0:T(8,128)(2,1)} %get-tuple-element.27), channel_id=1, source_target_pairs={{0,2},{1,3},{2,0},{3,1},{4,6},{5,7},{6,4},{7,5},{8,10},{9,11},{10,... | collective-permute-start | bytes 1572872 | tf_op jit(solution)/shard_map/ppermute | solution.py:298
  30.7 17.2 %collective-permute-start.2 = (bf16[8,2,32,512]{3,2,1,0:T(8,128)(2,1)S(1)}, bf16[8,2,32,512]{3,2,1,0:T(8,128)(2,1)}, u32[]{:S(2)}, u32[]{:S(2)}) collective-permute-start(bf16[8,2,32,512]{3,2,1,0:T(8,128)(2,1)S(1)} %collective-permute-done.1.refs_2_), channel_id=1, source_target_pairs={{0,1},{1,0},{2,3},{3,2},{4,5},{5,4},{6,7},{7,6},{8,9},{9,8},{10,11... | collective-permute-start | bytes 1572872 | tf_op jit(solution)/shard_map/ppermute | solution.py:298
  35.5 19.6 %all-to-all-start.1 = ((bf16[16,32,512]{2,1,0:T(8,128)(2,1)}), bf16[16,32,512]{2,1,0:T(8,128)(2,1)S(1)}, u32[]{:S(2)}, u32[]{:S(2)}) async-start(bf16[16,32,512]{2,1,0:T(8,128)(2,1)} %shard_map.38), calls=%async_computation.1 | async-start | bytes 1048576 | tf_op jit(solution)/shard_map/all_to_all | solution.py:329
  40.2 10.6 %collective-permute-start.4 = (bf16[8,2,32,512]{3,2,1,0:T(8,128)(2,1)S(1)}, bf16[8,2,32,512]{3,2,1,0:T(8,128)(2,1)S(1)}, u32[]{:S(2)}, u32[]{:S(2)}) collective-permute-start(bf16[8,2,32,512]{3,2,1,0:T(8,128)(2,1)S(1)} %collective-permute-done.3.refs_4_), channel_id=1, source_target_pairs={{0,1},{1,0},{2,3},{3,2},{4,5},{5,4},{6,7},{7,6},{8,9},{9,8},{10,11... | collective-permute-start | bytes 1572872 | tf_op jit(solution)/shard_map/ppermute | solution.py:298
  40.5 11.1 %collective-permute-start.6 = (bf16[8,2,32,512]{3,2,1,0:T(8,128)(2,1)S(1)}, bf16[8,2,32,512]{3,2,1,0:T(8,128)(2,1)S(1)}, u32[]{:S(2)}, u32[]{:S(2)}) collective-permute-start(bf16[8,2,32,512]{3,2,1,0:T(8,128)(2,1)S(1)} %collective-permute-done.5.refs_6_), channel_id=1, source_target_pairs={{0,1},{1,0},{2,3},{3,2},{4,5},{5,4},{6,7},{7,6},{8,9},{9,8},{10,11... | collective-permute-start | bytes 1572872 | tf_op jit(solution)/shard_map/ppermute | solution.py:298
  43.8 12.4 %collective-permute-start.10 = (bf16[8,2,32,512]{3,2,1,0:T(8,128)(2,1)S(1)}, bf16[8,2,32,512]{3,2,1,0:T(8,128)(2,1)}, u32[]{:S(2)}, u32[]{:S(2)}) collective-permute-start(bf16[8,2,32,512]{3,2,1,0:T(8,128)(2,1)S(1)} %collective-permute-done.9.refs_10_), channel_id=1, source_target_pairs={{0,1},{1,0},{2,3},{3,2},{4,5},{5,4},{6,7},{7,6},{8,9},{9,8},{10,11... | collective-permute-start | bytes 1572872 | tf_op jit(solution)/shard_map/ppermute | solution.py:298
  47.9 8.4 %collective-permute-start.8 = (bf16[8,2,32,512]{3,2,1,0:T(8,128)(2,1)}, bf16[8,2,32,512]{3,2,1,0:T(8,128)(2,1)}, u32[]{:S(2)}, u32[]{:S(2)}) collective-permute-start(bf16[8,2,32,512]{3,2,1,0:T(8,128)(2,1)} %collective-permute-done.7.refs_8_), channel_id=1, source_target_pairs={{0,1},{1,0},{2,3},{3,2},{4,5},{5,4},{6,7},{7,6},{8,9},{9,8},{10,11... | collective-permute-start | bytes 1572872 | tf_op jit(solution)/shard_map/ppermute | solution.py:298
  47.9 8.4 %collective-permute-start.12 = (bf16[8,2,32,512]{3,2,1,0:T(8,128)(2,1)}, bf16[8,2,32,512]{3,2,1,0:T(8,128)(2,1)}, u32[]{:S(2)}, u32[]{:S(2)}) collective-permute-start(bf16[8,2,32,512]{3,2,1,0:T(8,128)(2,1)} %collective-permute-done.11.refs_12_), channel_id=1, source_target_pairs={{0,1},{1,0},{2,3},{3,2},{4,5},{5,4},{6,7},{7,6},{8,9},{9,8},{10,11... | collective-permute-start | bytes 1572872 | tf_op jit(solution)/shard_map/ppermute | solution.py:298
  51.6 17.3 %collective-permute-start.16 = (bf16[8,2,16,512]{3,2,1,0:T(8,128)(2,1)}, bf16[8,2,16,512]{3,2,1,0:T(8,128)(2,1)S(1)}, u32[]{:S(2)}, u32[]{:S(2)}) collective-permute-start(bf16[8,2,16,512]{3,2,1,0:T(8,128)(2,1)} %slice.30), channel_id=1, source_target_pairs={{0,4},{1,5},{2,6},{3,7},{4,8},{5,9},{6,10},{7,11},{8,12},{9,13},{1... | collective-permute-start | bytes 786440 | tf_op jit(solution)/shard_map/ppermute | solution.py:298
  52.4 16.5 %collective-permute-start.17 = (bf16[8,2,16,512]{3,2,1,0:T(8,128)(2,1)}, bf16[8,2,16,512]{3,2,1,0:T(8,128)(2,1)}, u32[]{:S(2)}, u32[]{:S(2)}) collective-permute-start(bf16[8,2,16,512]{3,2,1,0:T(8,128)(2,1)} %slice.31), channel_id=1, source_target_pairs={{0,12},{1,13},{2,14},{3,15},{4,0},{5,1},{6,2},{7,3},{8,4},{9,5},{1... | collective-permute-start | bytes 786440 | tf_op jit(solution)/shard_map/ppermute | solution.py:298
  56.3 1.0 %copy-start.1 = (bf16[8,2,32,512]{3,2,1,0:T(8,128)(2,1)S(1)}, bf16[8,2,32,512]{3,2,1,0:T(8,128)(2,1)}, u32[]{:S(2)}) copy-start(bf16[8,2,32,512]{3,2,1,0:T(8,128)(2,1)} %copy-done) | copy-start | bytes 1572868
  57.3 1.0 %copy-start.3 = (bf16[8,2,32,512]{3,2,1,0:T(8,128)(2,1)S(1)}, bf16[8,2,32,512]{3,2,1,0:T(8,128)(2,1)}, u32[]{:S(2)}) copy-start(bf16[8,2,32,512]{3,2,1,0:T(8,128)(2,1)} %copy-done.2) | copy-start | bytes 1572868
  69.0 2.1 %collective-permute-start.18 = (bf16[8,2,16,512]{3,2,1,0:T(8,128)(2,1)S(1)}, bf16[8,2,16,512]{3,2,1,0:T(8,128)(2,1)S(1)}, u32[]{:S(2)}, u32[]{:S(2)}) collective-permute-start(bf16[8,2,16,512]{3,2,1,0:T(8,128)(2,1)S(1)} %collective-permute-done.16.refs_0_), channel_id=1, source_target_pairs={{0,1},{1,0},{2,3},{3,2},{4,5},{5,4},{6,7},{7,6},{8,9},{9,8},{10,11... | collective-permute-start | bytes 786440 | tf_op jit(solution)/shard_map/ppermute | solution.py:298
  69.9 1.7 %collective-permute-start.19 = (bf16[8,2,16,512]{3,2,1,0:T(8,128)(2,1)}, bf16[8,2,16,512]{3,2,1,0:T(8,128)(2,1)S(1)}, u32[]{:S(2)}, u32[]{:S(2)}) collective-permute-start(bf16[8,2,16,512]{3,2,1,0:T(8,128)(2,1)} %collective-permute-done.17.refs_2_), channel_id=1, source_target_pairs={{0,1},{1,0},{2,3},{3,2},{4,5},{5,4},{6,7},{7,6},{8,9},{9,8},{10,11... | collective-permute-start | bytes 786440 | tf_op jit(solution)/shard_map/ppermute | solution.py:298
  (4 other events, 2.9 us)

commit v3 on v2

--- a/solution.py
+++ b/solution.py
@@ -127,19 +127,7 @@
         white_ref[g, SOURCES:] = dot(real, turn).astype(jnp.bfloat16)
 
 
-def scales(col, got, good):
-    return pl.pallas_call(
-        scales_kernel,
-        out_shape=(
-            jax.ShapeDtypeStruct((SEG, BLOCK), jnp.float32),
-            jax.ShapeDtypeStruct((len(GROUPS), 2 * SOURCES, GROUP), jnp.bfloat16),
-        ),
-        in_specs=[pl.BlockSpec(memory_space=pltpu.SMEM)] + [pl.BlockSpec(memory_space=pltpu.VMEM)] * 2,
-        compiler_params=pltpu.CompilerParams(vmem_limit_bytes=8 * MIB),
-    )(col, got, good)
-
-
-def cross_groups(pieces, first_group, scale_ref, white_ref, crossed, raw, right0, right1, left0, left1, sems):
+def cross_groups(pieces, first_group, scale_ref, white_ref, crossed, raw, right0, right1, left0, left1, sems, setup=None):
     copies = []
     for piece in pieces:
         for half in range(piece.shape[2] // HALF):
@@ -148,6 +136,8 @@
     for copy in copies:
         copy.start()
     groups = len(copies)
+    if setup is not None:
+        setup()
 
     def arrive(g):
         pltpu.make_async_copy(raw.at[g], raw.at[g], sems.at[g]).wait()
@@ -204,19 +194,28 @@
     ]
 
 
-def cross(pieces, scale, white):
+def cross(pieces, col, got, good):
+    count = len(pieces)
+
     def kernel(*refs):
-        scale_ref, white_ref, out_ref = refs[len(pieces) : len(pieces) + 3]
-        cross_groups(refs[: len(pieces)], 0, scale_ref, white_ref, out_ref, *refs[len(pieces) + 3 :])
+        col_ref, got_ref, good_ref, out_ref, scale_ref, white_ref = refs[count : count + 6]
+        setup = lambda: scales_kernel(col_ref, got_ref, good_ref, scale_ref, white_ref)
+        cross_groups(refs[:count], 0, scale_ref, white_ref, out_ref, *refs[count + 6 :], setup=setup)
 
     return pl.pallas_call(
         kernel,
-        out_shape=jax.ShapeDtypeStruct((SOURCES, EARLY * 2 * HALF, BLOCK), jnp.bfloat16),
-        in_specs=[pl.BlockSpec(memory_space=pl.ANY)] * len(pieces) + [pl.BlockSpec(memory_space=pltpu.VMEM)] * 2,
+        out_shape=(
+            jax.ShapeDtypeStruct((SOURCES, EARLY * 2 * HALF, BLOCK), jnp.bfloat16),
+            jax.ShapeDtypeStruct((SEG, BLOCK), jnp.float32),
+            jax.ShapeDtypeStruct((len(GROUPS), 2 * SOURCES, GROUP), jnp.bfloat16),
+        ),
+        in_specs=[pl.BlockSpec(memory_space=pl.ANY)] * count
+        + [pl.BlockSpec(memory_space=pltpu.SMEM)]
+        + [pl.BlockSpec(memory_space=pltpu.VMEM)] * 2,
         scratch_shapes=cross_scratch(EARLY),
-        compiler_params=pltpu.CompilerParams(vmem_limit_bytes=28 * MIB),
+        compiler_params=pltpu.CompilerParams(vmem_limit_bytes=16 * MIB),
         cost_estimate=pl.CostEstimate(flops=10**9, bytes_accessed=MIB, transcendentals=0),
-    )(*pieces, scale, white)
+    )(*pieces, col, got, good)
 
 
 def finish(pieces, early, scale, white, table):
@@ -259,7 +258,7 @@
             pltpu.SemaphoreType.DMA((2,)),
             *cross_scratch(late),
         ],
-        compiler_params=pltpu.CompilerParams(vmem_limit_bytes=26 * MIB),
+        compiler_params=pltpu.CompilerParams(vmem_limit_bytes=12 * MIB),
         cost_estimate=pl.CostEstimate(flops=5 * 10**9, bytes_accessed=5 * MIB, transcendentals=0),
     )(*pieces, early, scale, white, table)
 
@@ -327,10 +326,9 @@
     chosen = choose(lax.axis_index("row").reshape(1), pairing, by_row, partial)
     chosen, table = lax.optimization_barrier((chosen, lag_table(col.reshape(1))))
     got = lax.all_to_all(chosen, "col", 0, 0, tiled=True)
-    scale, white = scales(col.reshape(1), got, good)
 
     pair = lambda *mine: [piece for one in mine for piece in (one, sibling(one))]
-    early = cross(pair(x, a1, b1, c1, a2, b2, c2), scale, white)
+    early, scale, white = cross(pair(x, a1, b1, c1, a2, b2, c2), col.reshape(1), got, good)
     early, a3, b3 = lax.optimization_barrier((early, a3, b3))
     return finish(pair(a3, b3), early, scale, white, table)
 

time: 84.3 us -> 83.6 us (level)
    pallas_call x2 -> x1, Pallas kernels: 11.7 us -> 11 us  [cross(): pl.pallas_call(kernel, out_shape=(jax.ShapeDtypeStruct((SOURCES, EARLY *...]
  transfers between devices with their start and end apart: 22 -> 22, of which waited for: 4 -> 4; matrix products, arithmetic and copies ran while one was open for 5% -> 5% of each run, Pallas kernels for 19% -> 18%
where the time goes in v3:
time: 83.6 us; the launch traced here: 83.1 us
  starting transfers between devices  40.9 us (49%)
  Pallas kernels  27 us (32%)
  local copies, waits for them, and re-layouts  8.21 us (10%)
  waiting for transfers between devices  5.44 us (7%)
  other arithmetic  1.24 us (1%)
    ppermute x20, starting transfers between devices, send(): return lax.ppermute(value, axis, [(n, where(n)) for n in range(16)])  31.9 us
    pallas_call x1, Pallas kernels, finish(): pl.pallas_call(kernel, out_shape=jax.ShapeDtypeStruct((SOURCES, LAGS, BLO...  12 us
    pallas_call x1, Pallas kernels, cross(): pl.pallas_call(kernel, out_shape=(jax.ShapeDtypeStruct((SOURCES, EARLY *...  11 us
    ppermute x20, waiting for transfers between devices, send(): return lax.ppermute(value, axis, [(n, where(n)) for n in range(16)])  5.43 us
    unnamed x12, local copies, waits for them, and re-layouts  5.01 us
    all_to_all x1, starting transfers between devices, on_device(): got = lax.all_to_all(chosen, 'col', 0, 0, tiled=True)  4.75 us
    all_to_all x1, starting transfers between devices, spread(): lax.all_to_all(copies, axis, 0, 0, tiled=True, axis_index_groups=groups)  4.24 us
    slice x2, local copies, waits for them, and re-layouts, on_device(): high = lambda v: v[:, :, HALF:]  1.69 us
  transfers between devices with their start and end apart: 22, of which 4 were waited for; matrix products, arithmetic and copies ran while one was open for 5% of the time, Pallas kernels for 18%

profile of v3, /device:TPU:17, one launch (start us, length us, event | category | flops | bytes accessed | tf_op | source)
XLA Modules:
  0.0 83.1 jit_solution(283721684346823619)
XLA Ops:
  0.0 1.2 %collective-permute-start.1 = (bf16[8,2,32,512]{3,2,1,0:T(8,128)(2,1)}, bf16[8,2,32,512]{3,2,1,0:T(8,128)(2,1)S(1)}, u32[]{:S(2)}, u32[]{:S(2)}) collective-permute-start(bf16[8,2,32,512]{3,2,1,0:T(8,128)(2,1)} %refs_0_.1), channel_id=1, source_target_pairs={{0,4},{1,5},{2,6},{3,7},{4,8},{5,9},{6,10},{7,11},{8,12},{9,13},{1... | collective-permute-start | bytes 1572872 | tf_op jit(solution)/shard_map/ppermute | solution.py:297
  1.2 1.6 %collective-permute-start.5 = (bf16[8,2,32,512]{3,2,1,0:T(8,128)(2,1)}, bf16[8,2,32,512]{3,2,1,0:T(8,128)(2,1)S(1)}, u32[]{:S(2)}, u32[]{:S(2)}) collective-permute-start(bf16[8,2,32,512]{3,2,1,0:T(8,128)(2,1)} %refs_0_.1), channel_id=1, source_target_pairs={{0,2},{1,3},{2,0},{3,1},{4,6},{5,7},{6,4},{7,5},{8,10},{9,11},{10,... | collective-permute-start | bytes 1572872 | tf_op jit(solution)/shard_map/ppermute | solution.py:297
  2.9 1.5 %collective-permute-start.3 = (bf16[8,2,32,512]{3,2,1,0:T(8,128)(2,1)}, bf16[8,2,32,512]{3,2,1,0:T(8,128)(2,1)S(1)}, u32[]{:S(2)}, u32[]{:S(2)}) collective-permute-start(bf16[8,2,32,512]{3,2,1,0:T(8,128)(2,1)} %refs_0_.1), channel_id=1, source_target_pairs={{0,12},{1,13},{2,14},{3,15},{4,0},{5,1},{6,2},{7,3},{8,4},{9,5},{1... | collective-permute-start | bytes 1572872 | tf_op jit(solution)/shard_map/ppermute | solution.py:297
  5.0 1.3 %shard_map.37 = (bf16[16,512]{1,0:T(8,128)(2,1)S(1)}, bf16[16,512]{1,0:T(8,128)(2,1)S(1)}, f32[1,512]{1,0:T(1,128)S(1)}) custom-call(bf16[8,2,32,512]{3,2,1,0:T(8,128)(2,1)} %refs_0_.1, s32[1,512]{1,0:T(1,128)S(1)} %bitcast.8), custom_call_target="tpu_custom_call" | custom-call | tf_op jit(solution)/shard_map/pallas_call | solution.py:75
  6.3 3.0 %collective-permute-start.13 = (bf16[16,512]{1,0:T(8,128)(2,1)S(1)}, bf16[16,512]{1,0:T(8,128)(2,1)S(1)}, u32[]{:S(2)}, u32[]{:S(2)}) collective-permute-start(bf16[16,512]{1,0:T(8,128)(2,1)S(1)} %get-tuple-element.16), channel_id=1, source_target_pairs={{0,64},{16,80},{32,96},{48,112},{64,128},{80,144},{96,160},{112,17... | collective-permute-start | bytes 49160 | tf_op jit(solution)/shard_map/ppermute | solution.py:297
  9.3 4.2 %collective-permute-start.14 = (bf16[16,512]{1,0:T(8,128)(2,1)S(1)}, bf16[16,512]{1,0:T(8,128)(2,1)S(1)}, u32[]{:S(2)}, u32[]{:S(2)}) collective-permute-start(bf16[16,512]{1,0:T(8,128)(2,1)S(1)} %get-tuple-element.16), channel_id=1, source_target_pairs={{0,128},{16,144},{32,160},{48,176},{64,192},{80,208},{96,224},{112... | collective-permute-start | bytes 49160 | tf_op jit(solution)/shard_map/ppermute | solution.py:297
  14.2 6.0 %collective-permute-start.15 = (bf16[16,512]{1,0:T(8,128)(2,1)S(1)}, bf16[16,512]{1,0:T(8,128)(2,1)S(1)}, u32[]{:S(2)}, u32[]{:S(2)}) collective-permute-start(bf16[16,512]{1,0:T(8,128)(2,1)S(1)} %get-tuple-element.16), channel_id=1, source_target_pairs={{0,192},{16,208},{32,224},{48,240},{64,0},{80,16},{96,32},{112,48}... | collective-permute-start | bytes 49160 | tf_op jit(solution)/shard_map/ppermute | solution.py:297
  20.3 1.9 %collective-permute-start = (bf16[8,2,32,512]{3,2,1,0:T(8,128)(2,1)}, bf16[8,2,32,512]{3,2,1,0:T(8,128)(2,1)}, u32[]{:S(2)}, u32[]{:S(2)}) collective-permute-start(bf16[8,2,32,512]{3,2,1,0:T(8,128)(2,1)} %refs_0_.1), channel_id=1, source_target_pairs={{0,1},{1,0},{2,3},{3,2},{4,5},{5,4},{6,7},{7,6},{8,9},{9,8},{10,11... | collective-permute-start | bytes 1572872 | tf_op jit(solution)/shard_map/ppermute | solution.py:297
  22.3 1.2 %pad_maximum_fusion = (bf16[8,2,32,512]{3,2,1,0:T(8,128)(2,1)}, bf16[8,2,32,512]{3,2,1,0:T(8,128)(2,1)}, bf16[8,2,32,512]{3,2,1,0:T(8,128)(2,1)}) fusion(bf16[8,2,16,512]{3,2,1,0:T(8,128)(2,1)S(1)} %slice.26, bf16[8,2,16,512]{3,2,1,0:T(8,128)(2,1)S(1)} %slice.29, bf16[8,2,16,512]{3,2,1,0:T(8,128)(2,1)S(1)} %get-tuple-element.27, ...), kind=kLoop, calls=%fused_computation | loop fusion | flops 2621440 | bytes 2621440 | tf_op jit(solution)/shard_map/concatenate | solution.py:317
  23.5 1.3 %collective-permute-start.9 = (bf16[8,2,32,512]{3,2,1,0:T(8,128)(2,1)}, bf16[8,2,32,512]{3,2,1,0:T(8,128)(2,1)S(1)}, u32[]{:S(2)}, u32[]{:S(2)}) collective-permute-start(bf16[8,2,32,512]{3,2,1,0:T(8,128)(2,1)} %get-tuple-element.30), channel_id=1, source_target_pairs={{0,12},{1,13},{2,14},{3,15},{4,0},{5,1},{6,2},{7,3},{8,4},{9,5},{1... | collective-permute-start | bytes 1572872 | tf_op jit(solution)/shard_map/ppermute | solution.py:297
  25.5 4.2 %all-to-all-start = ((bf16[4,4,16,512]{3,2,1,0:T(8,128)(2,1)}), bf16[4,4,16,512]{3,2,1,0:T(8,128)(2,1)S(1)}, u32[]{:S(2)}, u32[]{:S(2)}) async-start(bf16[4,4,16,512]{3,2,1,0:T(8,128)(2,1)} %broadcast_in_dim.2), calls=%async_computation | async-start | bytes 524288 | tf_op jit(solution)/shard_map/all_to_all | solution.py:306
  30.7 1.4 %collective-permute-start.2 = (bf16[8,2,32,512]{3,2,1,0:T(8,128)(2,1)S(1)}, bf16[8,2,32,512]{3,2,1,0:T(8,128)(2,1)}, u32[]{:S(2)}, u32[]{:S(2)}) collective-permute-start(bf16[8,2,32,512]{3,2,1,0:T(8,128)(2,1)S(1)} %collective-permute-done.1.refs_2_), channel_id=1, source_target_pairs={{0,1},{1,0},{2,3},{3,2},{4,5},{5,4},{6,7},{7,6},{8,9},{9,8},{10,11... | collective-permute-start | bytes 1572872 | tf_op jit(solution)/shard_map/ppermute | solution.py:297
  32.1 1.2 %shard_map.39.refs_7_ = bf16[256,1024]{1,0:T(8,128)(2,1)S(1)} custom-call(s32[1]{0:T(128)} %bitcast.col_ref.refs_14_), custom_call_target="tpu_custom_call" | custom-call | flops 1000000 | bytes 10000 | tf_op jit(solution)/shard_map/pallas_call | solution.py:287
  34.0 1.5 %shard_map.38 = bf16[16,32,512]{2,1,0:T(8,128)(2,1)} custom-call(s32[1]{0:T(128)} %bitcast.1.row_ref, s32[1,16]{1,0:T(1,128)S(1)} %copy-done.5, bf16[4,4,16,512]{3,2,1,0:T(8,128)(2,1)S(1)} %all-to-all-done.gathered_ref, bf16[16,512]{1,0:T(8,128)(2,1)S(1)} %get-tuple-element.17.energy_ref), custom_call_target="tpu_custom_call" | custom-call | tf_op jit(solution)/shard_map/pallas_call | solution.py:92
  35.5 4.7 %all-to-all-start.1 = ((bf16[16,32,512]{2,1,0:T(8,128)(2,1)}), bf16[16,32,512]{2,1,0:T(8,128)(2,1)S(1)}, u32[]{:S(2)}, u32[]{:S(2)}) async-start(bf16[16,32,512]{2,1,0:T(8,128)(2,1)} %shard_map.38), calls=%async_computation.1 | async-start | bytes 1048576 | tf_op jit(solution)/shard_map/all_to_all | solution.py:328
  40.8 3.0 %collective-permute-done.7.refs_8_ = bf16[8,2,32,512]{3,2,1,0:T(8,128)(2,1)} collective-permute-done((bf16[8,2,32,512]{3,2,1,0:T(8,128)(2,1)}, bf16[8,2,32,512]{3,2,1,0:T(8,128)(2,1)}, u32[]{:S(2)}, u32[]{:S(2)}) %collective-permute-start.7) | collective-permute-done | bytes 524320 | tf_op jit(solution)/shard_map/ppermute | solution.py:297
  43.8 4.0 %collective-permute-start.10 = (bf16[8,2,32,512]{3,2,1,0:T(8,128)(2,1)S(1)}, bf16[8,2,32,512]{3,2,1,0:T(8,128)(2,1)}, u32[]{:S(2)}, u32[]{:S(2)}) collective-permute-start(bf16[8,2,32,512]{3,2,1,0:T(8,128)(2,1)S(1)} %collective-permute-done.9.refs_10_), channel_id=1, source_target_pairs={{0,1},{1,0},{2,3},{3,2},{4,5},{5,4},{6,7},{7,6},{8,9},{9,8},{10,11... | collective-permute-start | bytes 1572872 | tf_op jit(solution)/shard_map/ppermute | solution.py:297
  48.4 1.7 %slice.30 = bf16[8,2,16,512]{3,2,1,0:T(8,128)(2,1)} slice(bf16[8,2,32,512]{3,2,1,0:T(8,128)(2,1)} %collective-permute-done.7.refs_8_), slice={[0:8], [0:2], [16:32], [0:512]} | slice | bytes 524288 | tf_op jit(solution)/shard_map/slice | solution.py:316
  52.4 2.7 %collective-permute-start.17 = (bf16[8,2,16,512]{3,2,1,0:T(8,128)(2,1)}, bf16[8,2,16,512]{3,2,1,0:T(8,128)(2,1)}, u32[]{:S(2)}, u32[]{:S(2)}) collective-permute-start(bf16[8,2,16,512]{3,2,1,0:T(8,128)(2,1)} %slice.31), channel_id=1, source_target_pairs={{0,12},{1,13},{2,14},{3,15},{4,0},{5,1},{6,2},{7,3},{8,4},{9,5},{1... | collective-permute-start | bytes 786440 | tf_op jit(solution)/shard_map/ppermute | solution.py:297
  55.1 1.0 %copy-done.1 = bf16[8,2,32,512]{3,2,1,0:T(8,128)(2,1)S(1)} copy-done((bf16[8,2,32,512]{3,2,1,0:T(8,128)(2,1)S(1)}, bf16[8,2,32,512]{3,2,1,0:T(8,128)(2,1)}, u32[]{:S(2)}) %copy-start.1) | copy-done | bytes 524312
  56.2 1.0 %copy-done.3 = bf16[8,2,32,512]{3,2,1,0:T(8,128)(2,1)S(1)} copy-done((bf16[8,2,32,512]{3,2,1,0:T(8,128)(2,1)S(1)}, bf16[8,2,32,512]{3,2,1,0:T(8,128)(2,1)}, u32[]{:S(2)}) %copy-start.3) | copy-done | bytes 524312
  57.2 11.0 %shard_map.40 = (bf16[16,896,512]{2,1,0:T(8,128)(2,1)S(1)}, f32[8,512]{1,0:T(8,128)S(1)}, bf16[32,32,256]{2,1,0:T(8,128)(2,1)S(1)}) custom-call(bf16[8,2,32,512]{3,2,1,0:T(8,128)(2,1)} %refs_0_.1, bf16[8,2,32,512]{3,2,1,0:T(8,128)(2,1)} %collective-permute-done.refs_1_, bf16[8,2,32,512]{3,2,1,0:T(8,128)(2,1)S(1)} %collective-permute-done.1.refs_2_, ...), custom_call_target="tpu_custom_call" | custom-call | flops 1000000000 | bytes 1048576 | tf_op jit(solution)/shard_map/pallas_call | solution.py:205
  69.2 1.1 %collective-permute-done.18.refs_1_ = bf16[8,2,16,512]{3,2,1,0:T(8,128)(2,1)S(1)} collective-permute-done((bf16[8,2,16,512]{3,2,1,0:T(8,128)(2,1)S(1)}, bf16[8,2,16,512]{3,2,1,0:T(8,128)(2,1)S(1)}, u32[]{:S(2)}, u32[]{:S(2)}) %collective-permute-start.18) | collective-permute-done | bytes 262176 | tf_op jit(solution)/shard_map/ppermute | solution.py:297
  70.9 12.0 %shard_map.41 = bf16[16,256,512]{2,1,0:T(8,128)(2,1)} custom-call(bf16[8,2,16,512]{3,2,1,0:T(8,128)(2,1)S(1)} %collective-permute-done.16.refs_0_, bf16[8,2,16,512]{3,2,1,0:T(8,128)(2,1)S(1)} %collective-permute-done.18.refs_1_, bf16[8,2,16,512]{3,2,1,0:T(8,128)(2,1)} %collective-permute-done.17.refs_2_, ...), custom_call_target="tpu_custom_call" | custom-call | flops 5000000000 | bytes 5242880 | tf_op jit(solution)/shard_map/pallas_call | solution.py:249
  (45 shorter events, 8.9 us)
Async XLA Ops:
  0.0 14.2 %collective-permute-start.1 = (bf16[8,2,32,512]{3,2,1,0:T(8,128)(2,1)}, bf16[8,2,32,512]{3,2,1,0:T(8,128)(2,1)S(1)}, u32[]{:S(2)}, u32[]{:S(2)}) collective-permute-start(bf16[8,2,32,512]{3,2,1,0:T(8,128)(2,1)} %refs_0_.1), channel_id=1, source_target_pairs={{0,4},{1,5},{2,6},{3,7},{4,8},{5,9},{6,10},{7,11},{8,12},{9,13},{1... | collective-permute-start | bytes 1572872 | tf_op jit(solution)/shard_map/ppermute | solution.py:297
  1.2 19.0 %collective-permute-start.5 = (bf16[8,2,32,512]{3,2,1,0:T(8,128)(2,1)}, bf16[8,2,32,512]{3,2,1,0:T(8,128)(2,1)S(1)}, u32[]{:S(2)}, u32[]{:S(2)}) collective-permute-start(bf16[8,2,32,512]{3,2,1,0:T(8,128)(2,1)} %refs_0_.1), channel_id=1, source_target_pairs={{0,2},{1,3},{2,0},{3,1},{4,6},{5,7},{6,4},{7,5},{8,10},{9,11},{10,... | collective-permute-start | bytes 1572872 | tf_op jit(solution)/shard_map/ppermute | solution.py:297
  2.9 19.4 %collective-permute-start.3 = (bf16[8,2,32,512]{3,2,1,0:T(8,128)(2,1)}, bf16[8,2,32,512]{3,2,1,0:T(8,128)(2,1)S(1)}, u32[]{:S(2)}, u32[]{:S(2)}) collective-permute-start(bf16[8,2,32,512]{3,2,1,0:T(8,128)(2,1)} %refs_0_.1), channel_id=1, source_target_pairs={{0,12},{1,13},{2,14},{3,15},{4,0},{5,1},{6,2},{7,3},{8,4},{9,5},{1... | collective-permute-start | bytes 1572872 | tf_op jit(solution)/shard_map/ppermute | solution.py:297
  6.3 18.5 %collective-permute-start.13 = (bf16[16,512]{1,0:T(8,128)(2,1)S(1)}, bf16[16,512]{1,0:T(8,128)(2,1)S(1)}, u32[]{:S(2)}, u32[]{:S(2)}) collective-permute-start(bf16[16,512]{1,0:T(8,128)(2,1)S(1)} %get-tuple-element.16), channel_id=1, source_target_pairs={{0,64},{16,80},{32,96},{48,112},{64,128},{80,144},{96,160},{112,17... | collective-permute-start | bytes 49160 | tf_op jit(solution)/shard_map/ppermute | solution.py:297
  9.3 15.5 %collective-permute-start.14 = (bf16[16,512]{1,0:T(8,128)(2,1)S(1)}, bf16[16,512]{1,0:T(8,128)(2,1)S(1)}, u32[]{:S(2)}, u32[]{:S(2)}) collective-permute-start(bf16[16,512]{1,0:T(8,128)(2,1)S(1)} %get-tuple-element.16), channel_id=1, source_target_pairs={{0,128},{16,144},{32,160},{48,176},{64,192},{80,208},{96,224},{112... | collective-permute-start | bytes 49160 | tf_op jit(solution)/shard_map/ppermute | solution.py:297
  14.2 10.5 %collective-permute-start.15 = (bf16[16,512]{1,0:T(8,128)(2,1)S(1)}, bf16[16,512]{1,0:T(8,128)(2,1)S(1)}, u32[]{:S(2)}, u32[]{:S(2)}) collective-permute-start(bf16[16,512]{1,0:T(8,128)(2,1)S(1)} %get-tuple-element.16), channel_id=1, source_target_pairs={{0,192},{16,208},{32,224},{48,240},{64,0},{80,16},{96,32},{112,48}... | collective-permute-start | bytes 49160 | tf_op jit(solution)/shard_map/ppermute | solution.py:297
  20.3 19.9 %collective-permute-start = (bf16[8,2,32,512]{3,2,1,0:T(8,128)(2,1)}, bf16[8,2,32,512]{3,2,1,0:T(8,128)(2,1)}, u32[]{:S(2)}, u32[]{:S(2)}) collective-permute-start(bf16[8,2,32,512]{3,2,1,0:T(8,128)(2,1)} %refs_0_.1), channel_id=1, source_target_pairs={{0,1},{1,0},{2,3},{3,2},{4,5},{5,4},{6,7},{7,6},{8,9},{9,8},{10,11... | collective-permute-start | bytes 1572872 | tf_op jit(solution)/shard_map/ppermute | solution.py:297
  23.5 17.0 %collective-permute-start.9 = (bf16[8,2,32,512]{3,2,1,0:T(8,128)(2,1)}, bf16[8,2,32,512]{3,2,1,0:T(8,128)(2,1)S(1)}, u32[]{:S(2)}, u32[]{:S(2)}) collective-permute-start(bf16[8,2,32,512]{3,2,1,0:T(8,128)(2,1)} %get-tuple-element.30), channel_id=1, source_target_pairs={{0,12},{1,13},{2,14},{3,15},{4,0},{5,1},{6,2},{7,3},{8,4},{9,5},{1... | collective-permute-start | bytes 1572872 | tf_op jit(solution)/shard_map/ppermute | solution.py:297
  25.5 7.8 %all-to-all-start = ((bf16[4,4,16,512]{3,2,1,0:T(8,128)(2,1)}), bf16[4,4,16,512]{3,2,1,0:T(8,128)(2,1)S(1)}, u32[]{:S(2)}, u32[]{:S(2)}) async-start(bf16[4,4,16,512]{3,2,1,0:T(8,128)(2,1)} %broadcast_in_dim.2), calls=%async_computation | async-start | bytes 524288 | tf_op jit(solution)/shard_map/all_to_all | solution.py:306
  29.7 14.1 %collective-permute-start.7 = (bf16[8,2,32,512]{3,2,1,0:T(8,128)(2,1)}, bf16[8,2,32,512]{3,2,1,0:T(8,128)(2,1)}, u32[]{:S(2)}, u32[]{:S(2)}) collective-permute-start(bf16[8,2,32,512]{3,2,1,0:T(8,128)(2,1)} %get-tuple-element.31), channel_id=1, source_target_pairs={{0,4},{1,5},{2,6},{3,7},{4,8},{5,9},{6,10},{7,11},{8,12},{9,13},{1... | collective-permute-start | bytes 1572872 | tf_op jit(solution)/shard_map/ppermute | solution.py:297
  29.9 17.9 %collective-permute-start.11 = (bf16[8,2,32,512]{3,2,1,0:T(8,128)(2,1)}, bf16[8,2,32,512]{3,2,1,0:T(8,128)(2,1)}, u32[]{:S(2)}, u32[]{:S(2)}) collective-permute-start(bf16[8,2,32,512]{3,2,1,0:T(8,128)(2,1)} %get-tuple-element.29), channel_id=1, source_target_pairs={{0,2},{1,3},{2,0},{3,1},{4,6},{5,7},{6,4},{7,5},{8,10},{9,11},{10,... | collective-permute-start | bytes 1572872 | tf_op jit(solution)/shard_map/ppermute | solution.py:297
  30.7 17.2 %collective-permute-start.2 = (bf16[8,2,32,512]{3,2,1,0:T(8,128)(2,1)S(1)}, bf16[8,2,32,512]{3,2,1,0:T(8,128)(2,1)}, u32[]{:S(2)}, u32[]{:S(2)}) collective-permute-start(bf16[8,2,32,512]{3,2,1,0:T(8,128)(2,1)S(1)} %collective-permute-done.1.refs_2_), channel_id=1, source_target_pairs={{0,1},{1,0},{2,3},{3,2},{4,5},{5,4},{6,7},{7,6},{8,9},{9,8},{10,11... | collective-permute-start | bytes 1572872 | tf_op jit(solution)/shard_map/ppermute | solution.py:297
  35.5 19.6 %all-to-all-start.1 = ((bf16[16,32,512]{2,1,0:T(8,128)(2,1)}), bf16[16,32,512]{2,1,0:T(8,128)(2,1)S(1)}, u32[]{:S(2)}, u32[]{:S(2)}) async-start(bf16[16,32,512]{2,1,0:T(8,128)(2,1)} %shard_map.38), calls=%async_computation.1 | async-start | bytes 1048576 | tf_op jit(solution)/shard_map/all_to_all | solution.py:328
  40.2 10.6 %collective-permute-start.4 = (bf16[8,2,32,512]{3,2,1,0:T(8,128)(2,1)S(1)}, bf16[8,2,32,512]{3,2,1,0:T(8,128)(2,1)S(1)}, u32[]{:S(2)}, u32[]{:S(2)}) collective-permute-start(bf16[8,2,32,512]{3,2,1,0:T(8,128)(2,1)S(1)} %collective-permute-done.3.refs_4_), channel_id=1, source_target_pairs={{0,1},{1,0},{2,3},{3,2},{4,5},{5,4},{6,7},{7,6},{8,9},{9,8},{10,11... | collective-permute-start | bytes 1572872 | tf_op jit(solution)/shard_map/ppermute | solution.py:297
  40.5 11.1 %collective-permute-start.6 = (bf16[8,2,32,512]{3,2,1,0:T(8,128)(2,1)S(1)}, bf16[8,2,32,512]{3,2,1,0:T(8,128)(2,1)S(1)}, u32[]{:S(2)}, u32[]{:S(2)}) collective-permute-start(bf16[8,2,32,512]{3,2,1,0:T(8,128)(2,1)S(1)} %collective-permute-done.5.refs_6_), channel_id=1, source_target_pairs={{0,1},{1,0},{2,3},{3,2},{4,5},{5,4},{6,7},{7,6},{8,9},{9,8},{10,11... | collective-permute-start | bytes 1572872 | tf_op jit(solution)/shard_map/ppermute | solution.py:297
  43.8 11.3 %collective-permute-start.10 = (bf16[8,2,32,512]{3,2,1,0:T(8,128)(2,1)S(1)}, bf16[8,2,32,512]{3,2,1,0:T(8,128)(2,1)}, u32[]{:S(2)}, u32[]{:S(2)}) collective-permute-start(bf16[8,2,32,512]{3,2,1,0:T(8,128)(2,1)S(1)} %collective-permute-done.9.refs_10_), channel_id=1, source_target_pairs={{0,1},{1,0},{2,3},{3,2},{4,5},{5,4},{6,7},{7,6},{8,9},{9,8},{10,11... | collective-permute-start | bytes 1572872 | tf_op jit(solution)/shard_map/ppermute | solution.py:297
  47.9 7.2 %collective-permute-start.8 = (bf16[8,2,32,512]{3,2,1,0:T(8,128)(2,1)}, bf16[8,2,32,512]{3,2,1,0:T(8,128)(2,1)}, u32[]{:S(2)}, u32[]{:S(2)}) collective-permute-start(bf16[8,2,32,512]{3,2,1,0:T(8,128)(2,1)} %collective-permute-done.7.refs_8_), channel_id=1, source_target_pairs={{0,1},{1,0},{2,3},{3,2},{4,5},{5,4},{6,7},{7,6},{8,9},{9,8},{10,11... | collective-permute-start | bytes 1572872 | tf_op jit(solution)/shard_map/ppermute | solution.py:297
  47.9 7.2 %collective-permute-start.12 = (bf16[8,2,32,512]{3,2,1,0:T(8,128)(2,1)}, bf16[8,2,32,512]{3,2,1,0:T(8,128)(2,1)}, u32[]{:S(2)}, u32[]{:S(2)}) collective-permute-start(bf16[8,2,32,512]{3,2,1,0:T(8,128)(2,1)} %collective-permute-done.11.refs_12_), channel_id=1, source_target_pairs={{0,1},{1,0},{2,3},{3,2},{4,5},{5,4},{6,7},{7,6},{8,9},{9,8},{10,11... | collective-permute-start | bytes 1572872 | tf_op jit(solution)/shard_map/ppermute | solution.py:297
  51.6 16.6 %collective-permute-start.16 = (bf16[8,2,16,512]{3,2,1,0:T(8,128)(2,1)}, bf16[8,2,16,512]{3,2,1,0:T(8,128)(2,1)S(1)}, u32[]{:S(2)}, u32[]{:S(2)}) collective-permute-start(bf16[8,2,16,512]{3,2,1,0:T(8,128)(2,1)} %slice.30), channel_id=1, source_target_pairs={{0,4},{1,5},{2,6},{3,7},{4,8},{5,9},{6,10},{7,11},{8,12},{9,13},{1... | collective-permute-start | bytes 786440 | tf_op jit(solution)/shard_map/ppermute | solution.py:297
  52.4 15.8 %collective-permute-start.17 = (bf16[8,2,16,512]{3,2,1,0:T(8,128)(2,1)}, bf16[8,2,16,512]{3,2,1,0:T(8,128)(2,1)}, u32[]{:S(2)}, u32[]{:S(2)}) collective-permute-start(bf16[8,2,16,512]{3,2,1,0:T(8,128)(2,1)} %slice.31), channel_id=1, source_target_pairs={{0,12},{1,13},{2,14},{3,15},{4,0},{5,1},{6,2},{7,3},{8,4},{9,5},{1... | collective-permute-start | bytes 786440 | tf_op jit(solution)/shard_map/ppermute | solution.py:297
  55.1 1.0 %copy-start.1 = (bf16[8,2,32,512]{3,2,1,0:T(8,128)(2,1)S(1)}, bf16[8,2,32,512]{3,2,1,0:T(8,128)(2,1)}, u32[]{:S(2)}) copy-start(bf16[8,2,32,512]{3,2,1,0:T(8,128)(2,1)} %copy-done) | copy-start | bytes 1572868
  56.2 1.0 %copy-start.3 = (bf16[8,2,32,512]{3,2,1,0:T(8,128)(2,1)S(1)}, bf16[8,2,32,512]{3,2,1,0:T(8,128)(2,1)}, u32[]{:S(2)}) copy-start(bf16[8,2,32,512]{3,2,1,0:T(8,128)(2,1)} %copy-done.2) | copy-start | bytes 1572868
  68.2 2.1 %collective-permute-start.18 = (bf16[8,2,16,512]{3,2,1,0:T(8,128)(2,1)S(1)}, bf16[8,2,16,512]{3,2,1,0:T(8,128)(2,1)S(1)}, u32[]{:S(2)}, u32[]{:S(2)}) collective-permute-start(bf16[8,2,16,512]{3,2,1,0:T(8,128)(2,1)S(1)} %collective-permute-done.16.refs_0_), channel_id=1, source_target_pairs={{0,1},{1,0},{2,3},{3,2},{4,5},{5,4},{6,7},{7,6},{8,9},{9,8},{10,11... | collective-permute-start | bytes 786440 | tf_op jit(solution)/shard_map/ppermute | solution.py:297
  69.1 1.7 %collective-permute-start.19 = (bf16[8,2,16,512]{3,2,1,0:T(8,128)(2,1)}, bf16[8,2,16,512]{3,2,1,0:T(8,128)(2,1)S(1)}, u32[]{:S(2)}, u32[]{:S(2)}) collective-permute-start(bf16[8,2,16,512]{3,2,1,0:T(8,128)(2,1)} %collective-permute-done.17.refs_2_), channel_id=1, source_target_pairs={{0,1},{1,0},{2,3},{3,2},{4,5},{5,4},{6,7},{7,6},{8,9},{9,8},{10,11... | collective-permute-start | bytes 786440 | tf_op jit(solution)/shard_map/ppermute | solution.py:297
  (4 other events, 2.9 us)

commit v4 on v3

--- a/solution.py
+++ b/solution.py
@@ -53,8 +53,15 @@
     return (x + 4 - dx) % 4 * 4 + (z + dz) % 2 * 2 + (core + dc) % 2
 
 
-def prepare_kernel(x_ref, mask_ref, src_ref, energy_ref, good_ref):
-    mask = mask_ref[...].astype(jnp.float32)
+def prepare_kernel(x_ref, mask_ref, src_ref, energy_ref, good_ref, near, sem):
+    copy = pltpu.make_async_copy(mask_ref, near, sem)
+    copy.start()
+    sums = []
+    for seg in range(SEG):
+        value = x_ref[seg].astype(jnp.float32).reshape(4 * HALF, BLOCK)
+        sums.append(jnp.sum(value * value, axis=0, keepdims=True))
+    copy.wait()
+    mask = near[...].astype(jnp.float32)
     good_ref[...] = mask
     row = lax.broadcasted_iota(jnp.int32, (SOURCES, BLOCK), 0)
     col = lax.broadcasted_iota(jnp.int32, (SOURCES, BLOCK), 1)
@@ -62,10 +69,6 @@
     for half in range(2):
         part = x_ref[:, :, half * HALF : (half + 1) * HALF, :].reshape(GROUP, BLOCK)
         src_ref[:, half * GROUP : (half + 1) * GROUP] = dot(pick, part, ((1,), (1,))).astype(jnp.bfloat16)
-    sums = []
-    for seg in range(SEG):
-        value = x_ref[seg].astype(jnp.float32).reshape(4 * HALF, BLOCK)
-        sums.append(jnp.sum(value * value, axis=0, keepdims=True))
     energy = jnp.concatenate(sums, axis=0) * mask
     high = energy.astype(jnp.bfloat16).astype(jnp.float32)
     energy_ref[...] = jnp.concatenate([high, energy - high], axis=0).astype(jnp.bfloat16)
@@ -76,23 +79,31 @@
         prepare_kernel,
         out_shape=(jax.ShapeDtypeStruct((SOURCES, BLOCK), jnp.bfloat16),) * 2
         + (jax.ShapeDtypeStruct((1, BLOCK), jnp.float32),),
+        in_specs=[pl.BlockSpec(memory_space=pltpu.VMEM), pl.BlockSpec(memory_space=pl.ANY)],
+        scratch_shapes=[pltpu.VMEM((1, BLOCK), jnp.int32), pltpu.SemaphoreType.DMA],
         compiler_params=pltpu.CompilerParams(vmem_limit_bytes=16 * MIB),
     )(x, mask)
 
 
-def choose_kernel(row_ref, pairing_ref, gathered_ref, energy_ref, out_ref):
+def choose_kernel(row_ref, pairing_ref, gathered_ref, energy_ref, out_ref, near, sem):
+    copy = pltpu.make_async_copy(pairing_ref, near, sem)
+    copy.start()
+    for slot in range(16):
+        out_ref[slot, SOURCES:] = energy_ref[...]
+    copy.wait()
     row = row_ref[0]
     for slot in range(16):
-        block = pairing_ref[0, slot]
+        block = near[0, slot]
         out_ref[slot, :SOURCES] = gathered_ref[block % 4, (row // 4 + 4 - block // 4) % 4]
-        out_ref[slot, SOURCES:] = energy_ref[...]
 
 
 def choose(row, pairing, gathered, energy):
     return pl.pallas_call(
         choose_kernel,
         out_shape=jax.ShapeDtypeStruct((16, 2 * SOURCES, BLOCK), jnp.bfloat16),
-        in_specs=[pl.BlockSpec(memory_space=pltpu.SMEM)] * 2 + [pl.BlockSpec(memory_space=pltpu.VMEM)] * 2,
+        in_specs=[pl.BlockSpec(memory_space=pltpu.SMEM), pl.BlockSpec(memory_space=pl.ANY)]
+        + [pl.BlockSpec(memory_space=pltpu.VMEM)] * 2,
+        scratch_shapes=[pltpu.SMEM((1, 16), jnp.int32), pltpu.SemaphoreType.DMA],
         compiler_params=pltpu.CompilerParams(vmem_limit_bytes=8 * MIB),
     )(row, pairing, gathered, energy)
 

time: 83.6 us -> 83.6 us (level)
  no operation moved by 1% of the time
where the time goes in v4:
time: 83.6 us; the launch traced here: 83.1 us
  starting transfers between devices  41 us (49%)
  Pallas kernels  27.1 us (32%)
  local copies, waits for them, and re-layouts  8.21 us (10%)
  waiting for transfers between devices  5.26 us (6%)
  other arithmetic  1.24 us (1%)
    ppermute x20, starting transfers between devices, send(): return lax.ppermute(value, axis, [(n, where(n)) for n in range(16)])  32 us
    pallas_call x1, Pallas kernels, finish(): pl.pallas_call(kernel, out_shape=jax.ShapeDtypeStruct((SOURCES, LAGS, BLO...  12 us
    pallas_call x1, Pallas kernels, cross(): pl.pallas_call(kernel, out_shape=(jax.ShapeDtypeStruct((SOURCES, EARLY *...  11 us
    ppermute x20, waiting for transfers between devices, send(): return lax.ppermute(value, axis, [(n, where(n)) for n in range(16)])  5.25 us
    unnamed x12, local copies, waits for them, and re-layouts  5.01 us
    all_to_all x1, starting transfers between devices, on_device(): got = lax.all_to_all(chosen, 'col', 0, 0, tiled=True)  4.76 us
    all_to_all x1, starting transfers between devices, spread(): lax.all_to_all(copies, axis, 0, 0, tiled=True, axis_index_groups=groups)  4.24 us
    slice x2, local copies, waits for them, and re-layouts, on_device(): high = lambda v: v[:, :, HALF:]  1.69 us
  transfers between devices with their start and end apart: 22, of which 4 were waited for; matrix products, arithmetic and copies ran while one was open for 5% of the time, Pallas kernels for 18%

profile of v4, /device:TPU:17, one launch (start us, length us, event | category | flops | bytes accessed | tf_op | source)
XLA Modules:
  0.0 83.1 jit_solution(17930314723698377297)
XLA Ops:
  0.0 1.2 %collective-permute-start.1 = (bf16[8,2,32,512]{3,2,1,0:T(8,128)(2,1)}, bf16[8,2,32,512]{3,2,1,0:T(8,128)(2,1)S(1)}, u32[]{:S(2)}, u32[]{:S(2)}) collective-permute-start(bf16[8,2,32,512]{3,2,1,0:T(8,128)(2,1)} %refs_0_.1), channel_id=1, source_target_pairs={{0,4},{1,5},{2,6},{3,7},{4,8},{5,9},{6,10},{7,11},{8,12},{9,13},{1... | collective-permute-start | bytes 1572872 | tf_op jit(solution)/shard_map/ppermute | solution.py:308
  1.2 1.6 %collective-permute-start.5 = (bf16[8,2,32,512]{3,2,1,0:T(8,128)(2,1)}, bf16[8,2,32,512]{3,2,1,0:T(8,128)(2,1)S(1)}, u32[]{:S(2)}, u32[]{:S(2)}) collective-permute-start(bf16[8,2,32,512]{3,2,1,0:T(8,128)(2,1)} %refs_0_.1), channel_id=1, source_target_pairs={{0,2},{1,3},{2,0},{3,1},{4,6},{5,7},{6,4},{7,5},{8,10},{9,11},{10,... | collective-permute-start | bytes 1572872 | tf_op jit(solution)/shard_map/ppermute | solution.py:308
  2.9 1.5 %collective-permute-start.3 = (bf16[8,2,32,512]{3,2,1,0:T(8,128)(2,1)}, bf16[8,2,32,512]{3,2,1,0:T(8,128)(2,1)S(1)}, u32[]{:S(2)}, u32[]{:S(2)}) collective-permute-start(bf16[8,2,32,512]{3,2,1,0:T(8,128)(2,1)} %refs_0_.1), channel_id=1, source_target_pairs={{0,12},{1,13},{2,14},{3,15},{4,0},{5,1},{6,2},{7,3},{8,4},{9,5},{1... | collective-permute-start | bytes 1572872 | tf_op jit(solution)/shard_map/ppermute | solution.py:308
  5.0 1.4 %shard_map.37 = (bf16[16,512]{1,0:T(8,128)(2,1)S(1)}, bf16[16,512]{1,0:T(8,128)(2,1)S(1)}, f32[1,512]{1,0:T(1,128)S(1)}) custom-call(bf16[8,2,32,512]{3,2,1,0:T(8,128)(2,1)} %refs_0_.1, s32[1,512]{1,0:T(1,128)S(1)} %bitcast.8), custom_call_target="tpu_custom_call" | custom-call | tf_op jit(solution)/shard_map/pallas_call | solution.py:78
  6.4 3.1 %collective-permute-start.13 = (bf16[16,512]{1,0:T(8,128)(2,1)S(1)}, bf16[16,512]{1,0:T(8,128)(2,1)S(1)}, u32[]{:S(2)}, u32[]{:S(2)}) collective-permute-start(bf16[16,512]{1,0:T(8,128)(2,1)S(1)} %get-tuple-element.16), channel_id=1, source_target_pairs={{0,64},{16,80},{32,96},{48,112},{64,128},{80,144},{96,160},{112,17... | collective-permute-start | bytes 49160 | tf_op jit(solution)/shard_map/ppermute | solution.py:308
  9.4 4.2 %collective-permute-start.14 = (bf16[16,512]{1,0:T(8,128)(2,1)S(1)}, bf16[16,512]{1,0:T(8,128)(2,1)S(1)}, u32[]{:S(2)}, u32[]{:S(2)}) collective-permute-start(bf16[16,512]{1,0:T(8,128)(2,1)S(1)} %get-tuple-element.16), channel_id=1, source_target_pairs={{0,128},{16,144},{32,160},{48,176},{64,192},{80,208},{96,224},{112... | collective-permute-start | bytes 49160 | tf_op jit(solution)/shard_map/ppermute | solution.py:308
  14.2 6.0 %collective-permute-start.15 = (bf16[16,512]{1,0:T(8,128)(2,1)S(1)}, bf16[16,512]{1,0:T(8,128)(2,1)S(1)}, u32[]{:S(2)}, u32[]{:S(2)}) collective-permute-start(bf16[16,512]{1,0:T(8,128)(2,1)S(1)} %get-tuple-element.16), channel_id=1, source_target_pairs={{0,192},{16,208},{32,224},{48,240},{64,0},{80,16},{96,32},{112,48}... | collective-permute-start | bytes 49160 | tf_op jit(solution)/shard_map/ppermute | solution.py:308
  20.3 1.9 %collective-permute-start = (bf16[8,2,32,512]{3,2,1,0:T(8,128)(2,1)}, bf16[8,2,32,512]{3,2,1,0:T(8,128)(2,1)}, u32[]{:S(2)}, u32[]{:S(2)}) collective-permute-start(bf16[8,2,32,512]{3,2,1,0:T(8,128)(2,1)} %refs_0_.1), channel_id=1, source_target_pairs={{0,1},{1,0},{2,3},{3,2},{4,5},{5,4},{6,7},{7,6},{8,9},{9,8},{10,11... | collective-permute-start | bytes 1572872 | tf_op jit(solution)/shard_map/ppermute | solution.py:308
  22.3 1.2 %pad_maximum_fusion = (bf16[8,2,32,512]{3,2,1,0:T(8,128)(2,1)}, bf16[8,2,32,512]{3,2,1,0:T(8,128)(2,1)}, bf16[8,2,32,512]{3,2,1,0:T(8,128)(2,1)}) fusion(bf16[8,2,16,512]{3,2,1,0:T(8,128)(2,1)S(1)} %slice.26, bf16[8,2,16,512]{3,2,1,0:T(8,128)(2,1)S(1)} %slice.29, bf16[8,2,16,512]{3,2,1,0:T(8,128)(2,1)S(1)} %get-tuple-element.27, ...), kind=kLoop, calls=%fused_computation | loop fusion | flops 2621440 | bytes 2621440 | tf_op jit(solution)/shard_map/concatenate | solution.py:328
  23.5 1.3 %collective-permute-start.9 = (bf16[8,2,32,512]{3,2,1,0:T(8,128)(2,1)}, bf16[8,2,32,512]{3,2,1,0:T(8,128)(2,1)S(1)}, u32[]{:S(2)}, u32[]{:S(2)}) collective-permute-start(bf16[8,2,32,512]{3,2,1,0:T(8,128)(2,1)} %get-tuple-element.30), channel_id=1, source_target_pairs={{0,12},{1,13},{2,14},{3,15},{4,0},{5,1},{6,2},{7,3},{8,4},{9,5},{1... | collective-permute-start | bytes 1572872 | tf_op jit(solution)/shard_map/ppermute | solution.py:308
  25.5 4.2 %all-to-all-start = ((bf16[4,4,16,512]{3,2,1,0:T(8,128)(2,1)}), bf16[4,4,16,512]{3,2,1,0:T(8,128)(2,1)S(1)}, u32[]{:S(2)}, u32[]{:S(2)}) async-start(bf16[4,4,16,512]{3,2,1,0:T(8,128)(2,1)} %broadcast_in_dim.2), calls=%async_computation | async-start | bytes 524288 | tf_op jit(solution)/shard_map/all_to_all | solution.py:317
  30.7 1.4 %collective-permute-start.2 = (bf16[8,2,32,512]{3,2,1,0:T(8,128)(2,1)S(1)}, bf16[8,2,32,512]{3,2,1,0:T(8,128)(2,1)}, u32[]{:S(2)}, u32[]{:S(2)}) collective-permute-start(bf16[8,2,32,512]{3,2,1,0:T(8,128)(2,1)S(1)} %collective-permute-done.1.refs_2_), channel_id=1, source_target_pairs={{0,1},{1,0},{2,3},{3,2},{4,5},{5,4},{6,7},{7,6},{8,9},{9,8},{10,11... | collective-permute-start | bytes 1572872 | tf_op jit(solution)/shard_map/ppermute | solution.py:308
  32.1 1.2 %shard_map.39.refs_7_ = bf16[256,1024]{1,0:T(8,128)(2,1)S(1)} custom-call(s32[1]{0:T(128)} %bitcast.col_ref.refs_14_), custom_call_target="tpu_custom_call" | custom-call | flops 1000000 | bytes 10000 | tf_op jit(solution)/shard_map/pallas_call | solution.py:298
  34.0 1.5 %shard_map.38 = bf16[16,32,512]{2,1,0:T(8,128)(2,1)} custom-call(s32[1]{0:T(128)} %bitcast.1.row_ref, s32[1,16]{1,0:T(1,128)S(1)} %copy-done.5, bf16[4,4,16,512]{3,2,1,0:T(8,128)(2,1)S(1)} %all-to-all-done.gathered_ref, bf16[16,512]{1,0:T(8,128)(2,1)S(1)} %get-tuple-element.17.energy_ref), custom_call_target="tpu_custom_call" | custom-call | tf_op jit(solution)/shard_map/pallas_call | solution.py:101
  35.5 4.8 %all-to-all-start.1 = ((bf16[16,32,512]{2,1,0:T(8,128)(2,1)}), bf16[16,32,512]{2,1,0:T(8,128)(2,1)S(1)}, u32[]{:S(2)}, u32[]{:S(2)}) async-start(bf16[16,32,512]{2,1,0:T(8,128)(2,1)} %shard_map.38), calls=%async_computation.1 | async-start | bytes 1048576 | tf_op jit(solution)/shard_map/all_to_all | solution.py:339
  40.8 3.0 %collective-permute-done.7.refs_8_ = bf16[8,2,32,512]{3,2,1,0:T(8,128)(2,1)} collective-permute-done((bf16[8,2,32,512]{3,2,1,0:T(8,128)(2,1)}, bf16[8,2,32,512]{3,2,1,0:T(8,128)(2,1)}, u32[]{:S(2)}, u32[]{:S(2)}) %collective-permute-start.7) | collective-permute-done | bytes 524320 | tf_op jit(solution)/shard_map/ppermute | solution.py:308
  43.8 4.0 %collective-permute-start.10 = (bf16[8,2,32,512]{3,2,1,0:T(8,128)(2,1)S(1)}, bf16[8,2,32,512]{3,2,1,0:T(8,128)(2,1)}, u32[]{:S(2)}, u32[]{:S(2)}) collective-permute-start(bf16[8,2,32,512]{3,2,1,0:T(8,128)(2,1)S(1)} %collective-permute-done.9.refs_10_), channel_id=1, source_target_pairs={{0,1},{1,0},{2,3},{3,2},{4,5},{5,4},{6,7},{7,6},{8,9},{9,8},{10,11... | collective-permute-start | bytes 1572872 | tf_op jit(solution)/shard_map/ppermute | solution.py:308
  48.4 1.7 %slice.30 = bf16[8,2,16,512]{3,2,1,0:T(8,128)(2,1)} slice(bf16[8,2,32,512]{3,2,1,0:T(8,128)(2,1)} %collective-permute-done.7.refs_8_), slice={[0:8], [0:2], [16:32], [0:512]} | slice | bytes 524288 | tf_op jit(solution)/shard_map/slice | solution.py:327
  52.4 2.7 %collective-permute-start.17 = (bf16[8,2,16,512]{3,2,1,0:T(8,128)(2,1)}, bf16[8,2,16,512]{3,2,1,0:T(8,128)(2,1)}, u32[]{:S(2)}, u32[]{:S(2)}) collective-permute-start(bf16[8,2,16,512]{3,2,1,0:T(8,128)(2,1)} %slice.31), channel_id=1, source_target_pairs={{0,12},{1,13},{2,14},{3,15},{4,0},{5,1},{6,2},{7,3},{8,4},{9,5},{1... | collective-permute-start | bytes 786440 | tf_op jit(solution)/shard_map/ppermute | solution.py:308
  55.1 1.0 %copy-done.1 = bf16[8,2,32,512]{3,2,1,0:T(8,128)(2,1)S(1)} copy-done((bf16[8,2,32,512]{3,2,1,0:T(8,128)(2,1)S(1)}, bf16[8,2,32,512]{3,2,1,0:T(8,128)(2,1)}, u32[]{:S(2)}) %copy-start.1) | copy-done | bytes 524312
  56.1 1.0 %copy-done.3 = bf16[8,2,32,512]{3,2,1,0:T(8,128)(2,1)S(1)} copy-done((bf16[8,2,32,512]{3,2,1,0:T(8,128)(2,1)S(1)}, bf16[8,2,32,512]{3,2,1,0:T(8,128)(2,1)}, u32[]{:S(2)}) %copy-start.3) | copy-done | bytes 524312
  57.2 11.0 %shard_map.40 = (bf16[16,896,512]{2,1,0:T(8,128)(2,1)S(1)}, f32[8,512]{1,0:T(8,128)S(1)}, bf16[32,32,256]{2,1,0:T(8,128)(2,1)S(1)}) custom-call(bf16[8,2,32,512]{3,2,1,0:T(8,128)(2,1)} %refs_0_.1, bf16[8,2,32,512]{3,2,1,0:T(8,128)(2,1)} %collective-permute-done.refs_1_, bf16[8,2,32,512]{3,2,1,0:T(8,128)(2,1)S(1)} %collective-permute-done.1.refs_2_, ...), custom_call_target="tpu_custom_call" | custom-call | flops 1000000000 | bytes 1048576 | tf_op jit(solution)/shard_map/pallas_call | solution.py:216
  69.2 1.1 %collective-permute-done.18.refs_1_ = bf16[8,2,16,512]{3,2,1,0:T(8,128)(2,1)S(1)} collective-permute-done((bf16[8,2,16,512]{3,2,1,0:T(8,128)(2,1)S(1)}, bf16[8,2,16,512]{3,2,1,0:T(8,128)(2,1)S(1)}, u32[]{:S(2)}, u32[]{:S(2)}) %collective-permute-start.18) | collective-permute-done | bytes 262176 | tf_op jit(solution)/shard_map/ppermute | solution.py:308
  70.9 12.0 %shard_map.41 = bf16[16,256,512]{2,1,0:T(8,128)(2,1)} custom-call(bf16[8,2,16,512]{3,2,1,0:T(8,128)(2,1)S(1)} %collective-permute-done.16.refs_0_, bf16[8,2,16,512]{3,2,1,0:T(8,128)(2,1)S(1)} %collective-permute-done.18.refs_1_, bf16[8,2,16,512]{3,2,1,0:T(8,128)(2,1)} %collective-permute-done.17.refs_2_, ...), custom_call_target="tpu_custom_call" | custom-call | flops 5000000000 | bytes 5242880 | tf_op jit(solution)/shard_map/pallas_call | solution.py:260
  (45 shorter events, 8.7 us)
Async XLA Ops:
  0.0 14.2 %collective-permute-start.1 = (bf16[8,2,32,512]{3,2,1,0:T(8,128)(2,1)}, bf16[8,2,32,512]{3,2,1,0:T(8,128)(2,1)S(1)}, u32[]{:S(2)}, u32[]{:S(2)}) collective-permute-start(bf16[8,2,32,512]{3,2,1,0:T(8,128)(2,1)} %refs_0_.1), channel_id=1, source_target_pairs={{0,4},{1,5},{2,6},{3,7},{4,8},{5,9},{6,10},{7,11},{8,12},{9,13},{1... | collective-permute-start | bytes 1572872 | tf_op jit(solution)/shard_map/ppermute | solution.py:308
  1.2 19.0 %collective-permute-start.5 = (bf16[8,2,32,512]{3,2,1,0:T(8,128)(2,1)}, bf16[8,2,32,512]{3,2,1,0:T(8,128)(2,1)S(1)}, u32[]{:S(2)}, u32[]{:S(2)}) collective-permute-start(bf16[8,2,32,512]{3,2,1,0:T(8,128)(2,1)} %refs_0_.1), channel_id=1, source_target_pairs={{0,2},{1,3},{2,0},{3,1},{4,6},{5,7},{6,4},{7,5},{8,10},{9,11},{10,... | collective-permute-start | bytes 1572872 | tf_op jit(solution)/shard_map/ppermute | solution.py:308
  2.9 19.4 %collective-permute-start.3 = (bf16[8,2,32,512]{3,2,1,0:T(8,128)(2,1)}, bf16[8,2,32,512]{3,2,1,0:T(8,128)(2,1)S(1)}, u32[]{:S(2)}, u32[]{:S(2)}) collective-permute-start(bf16[8,2,32,512]{3,2,1,0:T(8,128)(2,1)} %refs_0_.1), channel_id=1, source_target_pairs={{0,12},{1,13},{2,14},{3,15},{4,0},{5,1},{6,2},{7,3},{8,4},{9,5},{1... | collective-permute-start | bytes 1572872 | tf_op jit(solution)/shard_map/ppermute | solution.py:308
  6.4 18.4 %collective-permute-start.13 = (bf16[16,512]{1,0:T(8,128)(2,1)S(1)}, bf16[16,512]{1,0:T(8,128)(2,1)S(1)}, u32[]{:S(2)}, u32[]{:S(2)}) collective-permute-start(bf16[16,512]{1,0:T(8,128)(2,1)S(1)} %get-tuple-element.16), channel_id=1, source_target_pairs={{0,64},{16,80},{32,96},{48,112},{64,128},{80,144},{96,160},{112,17... | collective-permute-start | bytes 49160 | tf_op jit(solution)/shard_map/ppermute | solution.py:308
  9.4 15.3 %collective-permute-start.14 = (bf16[16,512]{1,0:T(8,128)(2,1)S(1)}, bf16[16,512]{1,0:T(8,128)(2,1)S(1)}, u32[]{:S(2)}, u32[]{:S(2)}) collective-permute-start(bf16[16,512]{1,0:T(8,128)(2,1)S(1)} %get-tuple-element.16), channel_id=1, source_target_pairs={{0,128},{16,144},{32,160},{48,176},{64,192},{80,208},{96,224},{112... | collective-permute-start | bytes 49160 | tf_op jit(solution)/shard_map/ppermute | solution.py:308
  14.2 10.5 %collective-permute-start.15 = (bf16[16,512]{1,0:T(8,128)(2,1)S(1)}, bf16[16,512]{1,0:T(8,128)(2,1)S(1)}, u32[]{:S(2)}, u32[]{:S(2)}) collective-permute-start(bf16[16,512]{1,0:T(8,128)(2,1)S(1)} %get-tuple-element.16), channel_id=1, source_target_pairs={{0,192},{16,208},{32,224},{48,240},{64,0},{80,16},{96,32},{112,48}... | collective-permute-start | bytes 49160 | tf_op jit(solution)/shard_map/ppermute | solution.py:308
  20.3 20.0 %collective-permute-start = (bf16[8,2,32,512]{3,2,1,0:T(8,128)(2,1)}, bf16[8,2,32,512]{3,2,1,0:T(8,128)(2,1)}, u32[]{:S(2)}, u32[]{:S(2)}) collective-permute-start(bf16[8,2,32,512]{3,2,1,0:T(8,128)(2,1)} %refs_0_.1), channel_id=1, source_target_pairs={{0,1},{1,0},{2,3},{3,2},{4,5},{5,4},{6,7},{7,6},{8,9},{9,8},{10,11... | collective-permute-start | bytes 1572872 | tf_op jit(solution)/shard_map/ppermute | solution.py:308
  23.5 17.1 %collective-permute-start.9 = (bf16[8,2,32,512]{3,2,1,0:T(8,128)(2,1)}, bf16[8,2,32,512]{3,2,1,0:T(8,128)(2,1)S(1)}, u32[]{:S(2)}, u32[]{:S(2)}) collective-permute-start(bf16[8,2,32,512]{3,2,1,0:T(8,128)(2,1)} %get-tuple-element.30), channel_id=1, source_target_pairs={{0,12},{1,13},{2,14},{3,15},{4,0},{5,1},{6,2},{7,3},{8,4},{9,5},{1... | collective-permute-start | bytes 1572872 | tf_op jit(solution)/shard_map/ppermute | solution.py:308
  25.5 7.8 %all-to-all-start = ((bf16[4,4,16,512]{3,2,1,0:T(8,128)(2,1)}), bf16[4,4,16,512]{3,2,1,0:T(8,128)(2,1)S(1)}, u32[]{:S(2)}, u32[]{:S(2)}) async-start(bf16[4,4,16,512]{3,2,1,0:T(8,128)(2,1)} %broadcast_in_dim.2), calls=%async_computation | async-start | bytes 524288 | tf_op jit(solution)/shard_map/all_to_all | solution.py:317
  29.7 14.1 %collective-permute-start.7 = (bf16[8,2,32,512]{3,2,1,0:T(8,128)(2,1)}, bf16[8,2,32,512]{3,2,1,0:T(8,128)(2,1)}, u32[]{:S(2)}, u32[]{:S(2)}) collective-permute-start(bf16[8,2,32,512]{3,2,1,0:T(8,128)(2,1)} %get-tuple-element.31), channel_id=1, source_target_pairs={{0,4},{1,5},{2,6},{3,7},{4,8},{5,9},{6,10},{7,11},{8,12},{9,13},{1... | collective-permute-start | bytes 1572872 | tf_op jit(solution)/shard_map/ppermute | solution.py:308
  29.9 17.9 %collective-permute-start.11 = (bf16[8,2,32,512]{3,2,1,0:T(8,128)(2,1)}, bf16[8,2,32,512]{3,2,1,0:T(8,128)(2,1)}, u32[]{:S(2)}, u32[]{:S(2)}) collective-permute-start(bf16[8,2,32,512]{3,2,1,0:T(8,128)(2,1)} %get-tuple-element.29), channel_id=1, source_target_pairs={{0,2},{1,3},{2,0},{3,1},{4,6},{5,7},{6,4},{7,5},{8,10},{9,11},{10,... | collective-permute-start | bytes 1572872 | tf_op jit(solution)/shard_map/ppermute | solution.py:308
  30.7 17.2 %collective-permute-start.2 = (bf16[8,2,32,512]{3,2,1,0:T(8,128)(2,1)S(1)}, bf16[8,2,32,512]{3,2,1,0:T(8,128)(2,1)}, u32[]{:S(2)}, u32[]{:S(2)}) collective-permute-start(bf16[8,2,32,512]{3,2,1,0:T(8,128)(2,1)S(1)} %collective-permute-done.1.refs_2_), channel_id=1, source_target_pairs={{0,1},{1,0},{2,3},{3,2},{4,5},{5,4},{6,7},{7,6},{8,9},{9,8},{10,11... | collective-permute-start | bytes 1572872 | tf_op jit(solution)/shard_map/ppermute | solution.py:308
  35.5 19.6 %all-to-all-start.1 = ((bf16[16,32,512]{2,1,0:T(8,128)(2,1)}), bf16[16,32,512]{2,1,0:T(8,128)(2,1)S(1)}, u32[]{:S(2)}, u32[]{:S(2)}) async-start(bf16[16,32,512]{2,1,0:T(8,128)(2,1)} %shard_map.38), calls=%async_computation.1 | async-start | bytes 1048576 | tf_op jit(solution)/shard_map/all_to_all | solution.py:339
  40.2 10.6 %collective-permute-start.4 = (bf16[8,2,32,512]{3,2,1,0:T(8,128)(2,1)S(1)}, bf16[8,2,32,512]{3,2,1,0:T(8,128)(2,1)S(1)}, u32[]{:S(2)}, u32[]{:S(2)}) collective-permute-start(bf16[8,2,32,512]{3,2,1,0:T(8,128)(2,1)S(1)} %collective-permute-done.3.refs_4_), channel_id=1, source_target_pairs={{0,1},{1,0},{2,3},{3,2},{4,5},{5,4},{6,7},{7,6},{8,9},{9,8},{10,11... | collective-permute-start | bytes 1572872 | tf_op jit(solution)/shard_map/ppermute | solution.py:308
  40.6 11.0 %collective-permute-start.6 = (bf16[8,2,32,512]{3,2,1,0:T(8,128)(2,1)S(1)}, bf16[8,2,32,512]{3,2,1,0:T(8,128)(2,1)S(1)}, u32[]{:S(2)}, u32[]{:S(2)}) collective-permute-start(bf16[8,2,32,512]{3,2,1,0:T(8,128)(2,1)S(1)} %collective-permute-done.5.refs_6_), channel_id=1, source_target_pairs={{0,1},{1,0},{2,3},{3,2},{4,5},{5,4},{6,7},{7,6},{8,9},{9,8},{10,11... | collective-permute-start | bytes 1572872 | tf_op jit(solution)/shard_map/ppermute | solution.py:308
  43.8 11.2 %collective-permute-start.10 = (bf16[8,2,32,512]{3,2,1,0:T(8,128)(2,1)S(1)}, bf16[8,2,32,512]{3,2,1,0:T(8,128)(2,1)}, u32[]{:S(2)}, u32[]{:S(2)}) collective-permute-start(bf16[8,2,32,512]{3,2,1,0:T(8,128)(2,1)S(1)} %collective-permute-done.9.refs_10_), channel_id=1, source_target_pairs={{0,1},{1,0},{2,3},{3,2},{4,5},{5,4},{6,7},{7,6},{8,9},{9,8},{10,11... | collective-permute-start | bytes 1572872 | tf_op jit(solution)/shard_map/ppermute | solution.py:308
  47.9 7.2 %collective-permute-start.8 = (bf16[8,2,32,512]{3,2,1,0:T(8,128)(2,1)}, bf16[8,2,32,512]{3,2,1,0:T(8,128)(2,1)}, u32[]{:S(2)}, u32[]{:S(2)}) collective-permute-start(bf16[8,2,32,512]{3,2,1,0:T(8,128)(2,1)} %collective-permute-done.7.refs_8_), channel_id=1, source_target_pairs={{0,1},{1,0},{2,3},{3,2},{4,5},{5,4},{6,7},{7,6},{8,9},{9,8},{10,11... | collective-permute-start | bytes 1572872 | tf_op jit(solution)/shard_map/ppermute | solution.py:308
  47.9 7.2 %collective-permute-start.12 = (bf16[8,2,32,512]{3,2,1,0:T(8,128)(2,1)}, bf16[8,2,32,512]{3,2,1,0:T(8,128)(2,1)}, u32[]{:S(2)}, u32[]{:S(2)}) collective-permute-start(bf16[8,2,32,512]{3,2,1,0:T(8,128)(2,1)} %collective-permute-done.11.refs_12_), channel_id=1, source_target_pairs={{0,1},{1,0},{2,3},{3,2},{4,5},{5,4},{6,7},{7,6},{8,9},{9,8},{10,11... | collective-permute-start | bytes 1572872 | tf_op jit(solution)/shard_map/ppermute | solution.py:308
  51.6 16.6 %collective-permute-start.16 = (bf16[8,2,16,512]{3,2,1,0:T(8,128)(2,1)}, bf16[8,2,16,512]{3,2,1,0:T(8,128)(2,1)S(1)}, u32[]{:S(2)}, u32[]{:S(2)}) collective-permute-start(bf16[8,2,16,512]{3,2,1,0:T(8,128)(2,1)} %slice.30), channel_id=1, source_target_pairs={{0,4},{1,5},{2,6},{3,7},{4,8},{5,9},{6,10},{7,11},{8,12},{9,13},{1... | collective-permute-start | bytes 786440 | tf_op jit(solution)/shard_map/ppermute | solution.py:308
  52.4 15.8 %collective-permute-start.17 = (bf16[8,2,16,512]{3,2,1,0:T(8,128)(2,1)}, bf16[8,2,16,512]{3,2,1,0:T(8,128)(2,1)}, u32[]{:S(2)}, u32[]{:S(2)}) collective-permute-start(bf16[8,2,16,512]{3,2,1,0:T(8,128)(2,1)} %slice.31), channel_id=1, source_target_pairs={{0,12},{1,13},{2,14},{3,15},{4,0},{5,1},{6,2},{7,3},{8,4},{9,5},{1... | collective-permute-start | bytes 786440 | tf_op jit(solution)/shard_map/ppermute | solution.py:308
  55.1 1.0 %copy-start.1 = (bf16[8,2,32,512]{3,2,1,0:T(8,128)(2,1)S(1)}, bf16[8,2,32,512]{3,2,1,0:T(8,128)(2,1)}, u32[]{:S(2)}) copy-start(bf16[8,2,32,512]{3,2,1,0:T(8,128)(2,1)} %copy-done) | copy-start | bytes 1572868
  56.1 1.0 %copy-start.3 = (bf16[8,2,32,512]{3,2,1,0:T(8,128)(2,1)S(1)}, bf16[8,2,32,512]{3,2,1,0:T(8,128)(2,1)}, u32[]{:S(2)}) copy-start(bf16[8,2,32,512]{3,2,1,0:T(8,128)(2,1)} %copy-done.2) | copy-start | bytes 1572868
  68.2 2.1 %collective-permute-start.18 = (bf16[8,2,16,512]{3,2,1,0:T(8,128)(2,1)S(1)}, bf16[8,2,16,512]{3,2,1,0:T(8,128)(2,1)S(1)}, u32[]{:S(2)}, u32[]{:S(2)}) collective-permute-start(bf16[8,2,16,512]{3,2,1,0:T(8,128)(2,1)S(1)} %collective-permute-done.16.refs_0_), channel_id=1, source_target_pairs={{0,1},{1,0},{2,3},{3,2},{4,5},{5,4},{6,7},{7,6},{8,9},{9,8},{10,11... | collective-permute-start | bytes 786440 | tf_op jit(solution)/shard_map/ppermute | solution.py:308
  69.1 1.7 %collective-permute-start.19 = (bf16[8,2,16,512]{3,2,1,0:T(8,128)(2,1)}, bf16[8,2,16,512]{3,2,1,0:T(8,128)(2,1)S(1)}, u32[]{:S(2)}, u32[]{:S(2)}) collective-permute-start(bf16[8,2,16,512]{3,2,1,0:T(8,128)(2,1)} %collective-permute-done.17.refs_2_), channel_id=1, source_target_pairs={{0,1},{1,0},{2,3},{3,2},{4,5},{5,4},{6,7},{7,6},{8,9},{9,8},{10,11... | collective-permute-start | bytes 786440 | tf_op jit(solution)/shard_map/ppermute | solution.py:308
  (4 other events, 2.9 us)
